TPU v7x, 256 devices: a whole 4x4x8 slice. The times are simulated.
256 devices in a mesh: tm: 64 (over x, y_lo, z), site: 4 (over y_hi, core).
Axes of the slice: x: 4, y: 4 (y_hi: 2, y_lo: 2; y = y_hi * 2 + y_lo), z: 8, core: 2. Of those that a mesh axis runs over, the one named last changes fastest.
Arguments:
- fields: int32 [64, 4096], P('tm', 'site'), may hold values 0 or 1
- bonds: int32 [4, 2048], replicated, may hold values 0 or 1
- source_sites: int32 [128], replicated, may hold values from 0 to 4095
- initial: float32 [64, 4096, 128], P('tm', 'site'), may hold values from -1.2 to 1.2
Outputs:
- solution: float32 [64, 4096, 128], P('tm', 'site')
- gradient: float32 [64, 4096, 128], P('tm', 'site')
All inputs are finite; a program needn't handle non-finite values. No bound on the sum of `fields` on one device may be relied on, other than what follows from the above.
Results may differ from a plain program's by a relative error of at most 0.00024.
Values sent between devices are 32-bit elements; how exact they have to be, the bound alone decides.
No kernel may reach another device: no remote copies, remote signals or barrier semaphores. Data moves between devices by JAX's collectives and lax.ppermute only.
A program may use at most 64 MiB of HBM per device.

v0:
```python
import jax
import jax.numpy as jnp
from jax import lax
from jax.sharding import PartitionSpec as P

LX = 64
LY = 64
PANEL = 128
ITERS = 6


coupling = 0.7368
hop_angle = 0.125


def with_halo(x, sides, width):
    for axis, dim in sides:
        size, length = (lax.axis_size(axis), x.shape[dim])
        up = [(i, (i + 1) % size) for i in range(size)]
        down = [(j, i) for i, j in up]
        last = lax.slice_in_dim(x, length - width, length, axis=dim)
        first = lax.slice_in_dim(x, 0, width, axis=dim)
        before = lax.ppermute(last, axis, up)
        after = lax.ppermute(first, axis, down)
        x = jnp.concatenate([before, x, after], axis=dim)
    return x


def shifted(value, axis, steps):
    count = lax.axis_size(axis)
    pairs = [(source, (source + steps) % count) for source in range(count)]
    return lax.ppermute(value, axis, pairs)


def rotate_pair(former, latter, hyper_cos, hyper_sin):
    return (hyper_cos * former + hyper_sin * latter, hyper_sin * former + hyper_cos * latter)


def hyper_tables(bonds):
    kept_bonds = bonds.astype(jnp.float32)
    angle_value = jnp.float32(hop_angle)
    return (1.0 + kept_bonds * (jnp.cosh(angle_value) - 1.0), kept_bonds * jnp.sinh(angle_value))


def bond_pairs_x(values, hyper_cos, hyper_sin):
    batch_count, row_count, site_count, column_count = values.shape
    paired = values.reshape(batch_count, row_count, site_count // 2, 2, column_count)
    former, latter = rotate_pair(
        paired[:, :, :, 0],
        paired[:, :, :, 1],
        hyper_cos[None, :, :, None],
        hyper_sin[None, :, :, None],
    )
    return jnp.stack([former, latter], axis=3).reshape(
        batch_count, row_count, site_count, column_count
    )


def shifted_pairs_x(values, hyper_cos, hyper_sin):
    rolled = jnp.roll(values, -1, axis=2)
    return jnp.roll(bond_pairs_x(rolled, hyper_cos, hyper_sin), 1, axis=2)


def bond_pairs_y(values, hyper_cos, hyper_sin):
    batch_count, row_count, site_count, column_count = values.shape
    paired = values.reshape(batch_count, row_count // 2, 2, site_count, column_count)
    former, latter = rotate_pair(
        paired[:, :, 0], paired[:, :, 1], hyper_cos[None, :, :, None], hyper_sin[None, :, :, None]
    )
    return jnp.stack([former, latter], axis=2).reshape(
        batch_count, row_count, site_count, column_count
    )


def strip_pairs(values, hyper_cos, hyper_sin):
    padded = with_halo(values, (("site", 1),), 1)
    joined = bond_pairs_y(padded, hyper_cos, hyper_sin)
    return joined[:, 1:-1]


def local_tables(bonds, strip_index, row_count):
    hyper_cos, hyper_sin = hyper_tables(bonds)
    half_rows = row_count // 2
    pair_rows = LY // 2
    tables = []
    for family in range(2):
        whole_cos = hyper_cos[family].reshape(LY, LX // 2)
        whole_sin = hyper_sin[family].reshape(LY, LX // 2)
        tables.append(
            (
                lax.dynamic_slice_in_dim(whole_cos, strip_index * row_count, row_count, 0),
                lax.dynamic_slice_in_dim(whole_sin, strip_index * row_count, row_count, 0),
            )
        )
    even_cos = hyper_cos[2].reshape(pair_rows, LX)
    even_sin = hyper_sin[2].reshape(pair_rows, LX)
    tables.append(
        (
            lax.dynamic_slice_in_dim(even_cos, strip_index * half_rows, half_rows, 0),
            lax.dynamic_slice_in_dim(even_sin, strip_index * half_rows, half_rows, 0),
        )
    )
    picked_rows = (
        strip_index * half_rows - 1 + jnp.arange(half_rows + 1, dtype=jnp.int32)
    ) % pair_rows
    odd_cos = hyper_cos[3].reshape(pair_rows, LX)
    odd_sin = hyper_sin[3].reshape(pair_rows, LX)
    tables.append((jnp.take(odd_cos, picked_rows, axis=0), jnp.take(odd_sin, picked_rows, axis=0)))
    return tables


def apply_slice_matrix(values, growth, tables):
    batch_count, sites_dev, column_count = values.shape
    row_count = growth.shape[1]
    lattice = values.reshape(batch_count, row_count, LX, column_count) * growth[..., None]
    lattice = bond_pairs_x(lattice, tables[0][0], tables[0][1])
    lattice = shifted_pairs_x(lattice, tables[1][0], tables[1][1])
    lattice = bond_pairs_y(lattice, tables[2][0], tables[2][1])
    lattice = strip_pairs(lattice, tables[3][0], tables[3][1])
    return lattice.reshape(batch_count, sites_dev, column_count)


def apply_transposed(values, growth, tables):
    batch_count, sites_dev, column_count = values.shape
    row_count = growth.shape[1]
    lattice = values.reshape(batch_count, row_count, LX, column_count)
    lattice = strip_pairs(lattice, tables[3][0], tables[3][1])
    lattice = bond_pairs_y(lattice, tables[2][0], tables[2][1])
    lattice = shifted_pairs_x(lattice, tables[1][0], tables[1][1])
    lattice = bond_pairs_x(lattice, tables[0][0], tables[0][1])
    lattice = lattice * growth[..., None]
    return lattice.reshape(batch_count, sites_dev, column_count)


def column_squares(values):
    return lax.psum(jnp.sum(values * values, axis=(0, 1)), ("tm", "site"))


def body(fields, bonds, source_sites, initial):
    slices_dev, sites_dev = fields.shape
    row_count = sites_dev // LX
    time_index = lax.axis_index("tm")
    strip_index = lax.axis_index("site")
    slice_total = slices_dev * lax.axis_size("tm")
    first_slice = time_index * slices_dev
    tables = local_tables(bonds, strip_index, row_count)
    column_ids = jnp.arange(PANEL, dtype=jnp.int32)
    source_slice = column_ids * slice_total // PANEL
    site_ids = strip_index * sites_dev + jnp.arange(sites_dev, dtype=jnp.int32)

    def loop_sign(slice_ids):
        return jnp.where(slice_ids == 0, 1.0, -1.0).astype(jnp.float32)[:, None, None]

    own_ids = first_slice + jnp.arange(slices_dev, dtype=jnp.int32)
    wide_ids = (first_slice + jnp.arange(slices_dev + 1, dtype=jnp.int32)) % slice_total
    growth = jnp.exp(coupling * (2.0 * fields.astype(jnp.float32) - 1.0)).reshape(
        fields.shape[0], row_count, LX
    )
    solution = initial
    own_sign = loop_sign(own_ids)
    next_sign = loop_sign(wide_ids[1:])

    def forward_product(values):
        arrived = shifted(values, "tm", 1)
        earlier = jnp.concatenate([arrived, values[:-1]], axis=0)
        return values + own_sign * apply_slice_matrix(earlier, growth, tables)

    def backward_product(values):
        image_now = apply_transposed(values, growth, tables)
        arrived = shifted(image_now, "tm", -1)
        later_terms = jnp.concatenate([image_now[1:], arrived], axis=0)
        return values + next_sign * later_terms

    matches = (own_ids[:, None, None] == source_slice[None, None, :]) & (
        site_ids[None, :, None] == source_sites[None, None, :]
    )
    residual = matches.astype(jnp.float32) - forward_product(initial)
    gradient = backward_product(residual)
    direction = gradient
    gamma_now = column_squares(gradient)
    for iteration in range(ITERS):
        image_now = forward_product(direction)
        step_size = (gamma_now / column_squares(image_now))[None, None, :]
        solution = solution + step_size * direction
        residual = residual - step_size * image_now
        gradient = backward_product(residual)
        if iteration + 1 < ITERS:
            gamma_next = column_squares(gradient)
            direction = gradient + (gamma_next / gamma_now)[None, None, :] * direction
            gamma_now = gamma_next
    return (solution, gradient)


def solution(mesh):
    placed = (P("tm", "site"), P(), P(), P("tm", "site", None))
    return jax.shard_map(
        body,
        mesh=mesh,
        in_specs=placed,
        out_specs=(P("tm", "site", None), P("tm", "site", None)),
        check_vma=False,
    )
```

profile of v0, /device:TPU:32, one launch (start us, length us, event | category | flops | bytes accessed | tf_op | source)
XLA Modules:
  0.0 1226.2 jit_solution(11298131059524903996)
XLA Ops:
  44.7 9.0 collective-permute-done.5
  53.9 14.0 %collective-permute-done.6 = f32[1,1024,128]{2,1,0:T(8,128)S(1)} collective-permute-done((f32[1,1024,128]{2,1,0:T(8,128)S(1)}, f32[1,1024,128]{2,1,0:T(8,128)S(1)}, u32[]{:S(2)}, u32[]{:S(2)}) %collective-permute-start.6) | collective-permute-done | bytes 524320 | tf_op jit(solution)/shard_map/ppermute | solution.py:32
  79.5 82.6 %all-reduce = (f32[128]{0:T(128)S(1)}, f32[128]{0:T(128)S(1)}) all-reduce(f32[128]{0:T(128)S(1)} %get-tuple-element.4, f32[128]{0:T(128)S(1)} %get-tuple-element.3), channel_id=1, replica_groups=mesh['tm'=64,'site'=4] {'tm','site'}, use_global_device_ids=true, to_apply=%region_1.3 | all-reduce | flops 256 | bytes 2048 | tf_op jit(solution)/shard_map/psum | solution.py:136
  172.1 14.3 %collective-permute-done.11 = f32[1,1024,128]{2,1,0:T(8,128)S(1)} collective-permute-done((f32[1,1024,128]{2,1,0:T(8,128)S(1)}, f32[1,1024,128]{2,1,0:T(8,128)S(1)}, u32[]{:S(2)}, u32[]{:S(2)}) %collective-permute-start.11) | collective-permute-done | bytes 524320 | tf_op jit(solution)/shard_map/ppermute | solution.py:32
  186.5 76.0 %psum.86 = f32[128]{0:T(128)S(1)} all-reduce(f32[128]{0:T(128)S(1)} %multiply_reduce_fusion.9), channel_id=1, replica_groups=mesh['tm'=64,'site'=4] {'tm','site'}, use_global_device_ids=true, to_apply=%region_5.7 | all-reduce | flops 128 | bytes 1024 | tf_op jit(solution)/shard_map/psum | solution.py:136
  263.9 13.1 %collective-permute-done.12 = f32[1,1024,128]{2,1,0:T(8,128)S(1)} collective-permute-done((f32[1,1024,128]{2,1,0:T(8,128)S(1)}, f32[1,1024,128]{2,1,0:T(8,128)S(1)}, u32[]{:S(2)}, u32[]{:S(2)}) %collective-permute-start.12) | collective-permute-done | bytes 524320 | tf_op jit(solution)/shard_map/ppermute | solution.py:32
  287.4 80.7 %psum.87 = f32[128]{0:T(128)S(1)} all-reduce(f32[128]{0:T(128)S(1)} %multiply_reduce_fusion.8), channel_id=1, replica_groups=mesh['tm'=64,'site'=4] {'tm','site'}, use_global_device_ids=true, to_apply=%region_7.9 | all-reduce | flops 128 | bytes 1024 | tf_op jit(solution)/shard_map/psum | solution.py:136
  378.1 14.5 %collective-permute-done.17 = f32[1,1024,128]{2,1,0:T(8,128)S(1)} collective-permute-done((f32[1,1024,128]{2,1,0:T(8,128)S(1)}, f32[1,1024,128]{2,1,0:T(8,128)S(1)}, u32[]{:S(2)}, u32[]{:S(2)}) %collective-permute-start.17) | collective-permute-done | bytes 524320 | tf_op jit(solution)/shard_map/ppermute | solution.py:32
  392.7 75.9 %psum.88 = f32[128]{0:T(128)S(1)} all-reduce(f32[128]{0:T(128)S(1)} %multiply_reduce_fusion.7), channel_id=1, replica_groups=mesh['tm'=64,'site'=4] {'tm','site'}, use_global_device_ids=true, to_apply=%region_9.11 | all-reduce | flops 128 | bytes 1024 | tf_op jit(solution)/shard_map/psum | solution.py:136
  469.6 12.9 %collective-permute-done.18 = f32[1,1024,128]{2,1,0:T(8,128)S(1)} collective-permute-done((f32[1,1024,128]{2,1,0:T(8,128)S(1)}, f32[1,1024,128]{2,1,0:T(8,128)S(1)}, u32[]{:S(2)}, u32[]{:S(2)}) %collective-permute-start.18) | collective-permute-done | bytes 524320 | tf_op jit(solution)/shard_map/ppermute | solution.py:32
  492.8 80.7 %psum.89 = f32[128]{0:T(128)S(1)} all-reduce(f32[128]{0:T(128)S(1)} %multiply_reduce_fusion.6), channel_id=1, replica_groups=mesh['tm'=64,'site'=4] {'tm','site'}, use_global_device_ids=true, to_apply=%region_11.13 | all-reduce | flops 128 | bytes 1024 | tf_op jit(solution)/shard_map/psum | solution.py:136
  583.5 14.5 %collective-permute-done.23 = f32[1,1024,128]{2,1,0:T(8,128)S(1)} collective-permute-done((f32[1,1024,128]{2,1,0:T(8,128)S(1)}, f32[1,1024,128]{2,1,0:T(8,128)S(1)}, u32[]{:S(2)}, u32[]{:S(2)}) %collective-permute-start.23) | collective-permute-done | bytes 524320 | tf_op jit(solution)/shard_map/ppermute | solution.py:32
  598.2 75.9 %psum.90 = f32[128]{0:T(128)S(1)} all-reduce(f32[128]{0:T(128)S(1)} %multiply_reduce_fusion.5), channel_id=1, replica_groups=mesh['tm'=64,'site'=4] {'tm','site'}, use_global_device_ids=true, to_apply=%region_13.15 | all-reduce | flops 128 | bytes 1024 | tf_op jit(solution)/shard_map/psum | solution.py:136
  675.2 12.9 %collective-permute-done.24 = f32[1,1024,128]{2,1,0:T(8,128)S(1)} collective-permute-done((f32[1,1024,128]{2,1,0:T(8,128)S(1)}, f32[1,1024,128]{2,1,0:T(8,128)S(1)}, u32[]{:S(2)}, u32[]{:S(2)}) %collective-permute-start.24) | collective-permute-done | bytes 524320 | tf_op jit(solution)/shard_map/ppermute | solution.py:32
  699.3 80.7 %psum.91 = f32[128]{0:T(128)S(1)} all-reduce(f32[128]{0:T(128)S(1)} %multiply_reduce_fusion.4), channel_id=1, replica_groups=mesh['tm'=64,'site'=4] {'tm','site'}, use_global_device_ids=true, to_apply=%region_15.17 | all-reduce | flops 128 | bytes 1024 | tf_op jit(solution)/shard_map/psum | solution.py:136
  791.0 14.5 %collective-permute-done.29 = f32[1,1024,128]{2,1,0:T(8,128)S(1)} collective-permute-done((f32[1,1024,128]{2,1,0:T(8,128)S(1)}, f32[1,1024,128]{2,1,0:T(8,128)S(1)}, u32[]{:S(2)}, u32[]{:S(2)}) %collective-permute-start.29) | collective-permute-done | bytes 524320 | tf_op jit(solution)/shard_map/ppermute | solution.py:32
  806.3 75.8 %psum.92 = f32[128]{0:T(128)S(1)} all-reduce(f32[128]{0:T(128)S(1)} %multiply_reduce_fusion.3), channel_id=1, replica_groups=mesh['tm'=64,'site'=4] {'tm','site'}, use_global_device_ids=true, to_apply=%region_17.19 | all-reduce | flops 128 | bytes 1024 | tf_op jit(solution)/shard_map/psum | solution.py:136
  884.2 12.9 %collective-permute-done.30 = f32[1,1024,128]{2,1,0:T(8,128)S(1)} collective-permute-done((f32[1,1024,128]{2,1,0:T(8,128)S(1)}, f32[1,1024,128]{2,1,0:T(8,128)S(1)}, u32[]{:S(2)}, u32[]{:S(2)}) %collective-permute-start.30) | collective-permute-done | bytes 524320 | tf_op jit(solution)/shard_map/ppermute | solution.py:32
  908.3 80.7 %psum.93 = f32[128]{0:T(128)S(1)} all-reduce(f32[128]{0:T(128)S(1)} %multiply_reduce_fusion.2), channel_id=1, replica_groups=mesh['tm'=64,'site'=4] {'tm','site'}, use_global_device_ids=true, to_apply=%region_19.21 | all-reduce | flops 128 | bytes 1024 | tf_op jit(solution)/shard_map/psum | solution.py:136
  1000.2 14.5 %collective-permute-done.35 = f32[1,1024,128]{2,1,0:T(8,128)S(1)} collective-permute-done((f32[1,1024,128]{2,1,0:T(8,128)S(1)}, f32[1,1024,128]{2,1,0:T(8,128)S(1)}, u32[]{:S(2)}, u32[]{:S(2)}) %collective-permute-start.35) | collective-permute-done | bytes 524320 | tf_op jit(solution)/shard_map/ppermute | solution.py:32
  1015.6 75.9 %psum.94 = f32[128]{0:T(128)S(1)} all-reduce(f32[128]{0:T(128)S(1)} %multiply_reduce_fusion.1), channel_id=1, replica_groups=mesh['tm'=64,'site'=4] {'tm','site'}, use_global_device_ids=true, to_apply=%region_21.23 | all-reduce | flops 128 | bytes 1024 | tf_op jit(solution)/shard_map/psum | solution.py:136
  1093.6 12.9 %collective-permute-done.36 = f32[1,1024,128]{2,1,0:T(8,128)S(1)} collective-permute-done((f32[1,1024,128]{2,1,0:T(8,128)S(1)}, f32[1,1024,128]{2,1,0:T(8,128)S(1)}, u32[]{:S(2)}, u32[]{:S(2)}) %collective-permute-start.36) | collective-permute-done | bytes 524320 | tf_op jit(solution)/shard_map/ppermute | solution.py:32
  1117.7 80.7 %psum.95 = f32[128]{0:T(128)S(1)} all-reduce(f32[128]{0:T(128)S(1)} %multiply_reduce_fusion), channel_id=1, replica_groups=mesh['tm'=64,'site'=4] {'tm','site'}, use_global_device_ids=true, to_apply=%region_23.25 | all-reduce | flops 128 | bytes 1024 | tf_op jit(solution)/shard_map/psum | solution.py:136
  1210.6 14.5 %collective-permute-done.41 = f32[1,1024,128]{2,1,0:T(8,128)S(1)} collective-permute-done((f32[1,1024,128]{2,1,0:T(8,128)S(1)}, f32[1,1024,128]{2,1,0:T(8,128)S(1)}, u32[]{:S(2)}, u32[]{:S(2)}) %collective-permute-start.41) | collective-permute-done | bytes 524320 | tf_op jit(solution)/shard_map/ppermute | solution.py:32
  (398 shorter events, 182.4 us)
Async XLA Ops:
  0.6 14.0 %collective-permute-start = (f32[1,1024,128]{2,1,0:T(8,128)}, f32[1,1024,128]{2,1,0:T(8,128)S(1)}, u32[]{:S(2)}, u32[]{:S(2)}) collective-permute-start(f32[1,1024,128]{2,1,0:T(8,128)} %param.9), channel_id=1, source_target_pairs={{0,4},{4,8},{8,12},{12,16},{16,20},{20,24},{24,28},{28,32},{32,36}... | collective-permute-start | bytes 1572872 | tf_op jit(solution)/shard_map/ppermute | solution.py:32
  19.5 4.9 collective-permute-start.1
  26.0 4.9 collective-permute-start.3
  35.9 17.7 %collective-permute-start.5 = (f32[1,1024,128]{2,1,0:T(8,128)S(1)}, f32[1,1024,128]{2,1,0:T(8,128)S(1)}, u32[]{:S(2)}, u32[]{:S(2)}) collective-permute-start(f32[1,1024,128]{2,1,0:T(8,128)S(1)} %broadcast_multiply_fusion.6), channel_id=1, source_target_pairs={{0,252},{4,0},{8,4},{12,8},{16,12},{20,16},{24,20},{28,24},{32,28}... | collective-permute-start | bytes 1572872 | tf_op jit(solution)/shard_map/ppermute | solution.py:32
  53.7 14.2 %collective-permute-start.6 = (f32[1,1024,128]{2,1,0:T(8,128)S(1)}, f32[1,1024,128]{2,1,0:T(8,128)S(1)}, u32[]{:S(2)}, u32[]{:S(2)}) collective-permute-start(f32[1,1024,128]{2,1,0:T(8,128)S(1)} %multiply_add_fusion.12), channel_id=1, source_target_pairs={{0,4},{4,8},{8,12},{12,16},{16,20},{20,24},{24,28},{28,32},{32,36}... | collective-permute-start | bytes 1572872 | tf_op jit(solution)/shard_map/ppermute | solution.py:32
  72.8 5.9 collective-permute-start.7
  74.0 5.0 collective-permute-start.8
  162.2 4.9 collective-permute-start.9
  172.0 14.4 %collective-permute-start.11 = (f32[1,1024,128]{2,1,0:T(8,128)S(1)}, f32[1,1024,128]{2,1,0:T(8,128)S(1)}, u32[]{:S(2)}, u32[]{:S(2)}) collective-permute-start(f32[1,1024,128]{2,1,0:T(8,128)S(1)} %broadcast_multiply_fusion.5), channel_id=1, source_target_pairs={{0,252},{4,0},{8,4},{12,8},{16,12},{20,16},{24,20},{28,24},{32,28}... | collective-permute-start | bytes 1572872 | tf_op jit(solution)/shard_map/ppermute | solution.py:32
  262.7 14.3 %collective-permute-start.12 = (f32[1,1024,128]{2,1,0:T(8,128)S(1)}, f32[1,1024,128]{2,1,0:T(8,128)S(1)}, u32[]{:S(2)}, u32[]{:S(2)}) collective-permute-start(f32[1,1024,128]{2,1,0:T(8,128)S(1)} %multiply_add_fusion.10), channel_id=1, source_target_pairs={{0,4},{4,8},{8,12},{12,16},{16,20},{20,24},{24,28},{28,32},{32,36}... | collective-permute-start | bytes 1572872 | tf_op jit(solution)/shard_map/ppermute | solution.py:32
  281.9 4.9 collective-permute-start.13
  368.2 4.9 collective-permute-start.15
  378.0 14.6 %collective-permute-start.17 = (f32[1,1024,128]{2,1,0:T(8,128)S(1)}, f32[1,1024,128]{2,1,0:T(8,128)S(1)}, u32[]{:S(2)}, u32[]{:S(2)}) collective-permute-start(f32[1,1024,128]{2,1,0:T(8,128)S(1)} %broadcast_multiply_fusion.4), channel_id=1, source_target_pairs={{0,252},{4,0},{8,4},{12,8},{16,12},{20,16},{24,20},{28,24},{32,28}... | collective-permute-start | bytes 1572872 | tf_op jit(solution)/shard_map/ppermute | solution.py:32
  468.7 13.8 %collective-permute-start.18 = (f32[1,1024,128]{2,1,0:T(8,128)S(1)}, f32[1,1024,128]{2,1,0:T(8,128)S(1)}, u32[]{:S(2)}, u32[]{:S(2)}) collective-permute-start(f32[1,1024,128]{2,1,0:T(8,128)S(1)} %multiply_add_fusion.8), channel_id=1, source_target_pairs={{0,4},{4,8},{8,12},{12,16},{16,20},{20,24},{24,28},{28,32},{32,36}... | collective-permute-start | bytes 1572872 | tf_op jit(solution)/shard_map/ppermute | solution.py:32
  487.4 4.9 collective-permute-start.19
  573.6 4.9 collective-permute-start.21
  583.4 14.6 %collective-permute-start.23 = (f32[1,1024,128]{2,1,0:T(8,128)S(1)}, f32[1,1024,128]{2,1,0:T(8,128)S(1)}, u32[]{:S(2)}, u32[]{:S(2)}) collective-permute-start(f32[1,1024,128]{2,1,0:T(8,128)S(1)} %broadcast_multiply_fusion.3), channel_id=1, source_target_pairs={{0,252},{4,0},{8,4},{12,8},{16,12},{20,16},{24,20},{28,24},{32,28}... | collective-permute-start | bytes 1572872 | tf_op jit(solution)/shard_map/ppermute | solution.py:32
  674.1 14.0 %collective-permute-start.24 = (f32[1,1024,128]{2,1,0:T(8,128)S(1)}, f32[1,1024,128]{2,1,0:T(8,128)S(1)}, u32[]{:S(2)}, u32[]{:S(2)}) collective-permute-start(f32[1,1024,128]{2,1,0:T(8,128)S(1)} %multiply_add_fusion.6), channel_id=1, source_target_pairs={{0,4},{4,8},{8,12},{12,16},{16,20},{20,24},{24,28},{28,32},{32,36}... | collective-permute-start | bytes 1572872 | tf_op jit(solution)/shard_map/ppermute | solution.py:32
  693.0 4.9 collective-permute-start.25
  790.9 14.6 %collective-permute-start.29 = (f32[1,1024,128]{2,1,0:T(8,128)S(1)}, f32[1,1024,128]{2,1,0:T(8,128)S(1)}, u32[]{:S(2)}, u32[]{:S(2)}) collective-permute-start(f32[1,1024,128]{2,1,0:T(8,128)S(1)} %broadcast_multiply_fusion.2), channel_id=1, source_target_pairs={{0,252},{4,0},{8,4},{12,8},{16,12},{20,16},{24,20},{28,24},{32,28}... | collective-permute-start | bytes 1572872 | tf_op jit(solution)/shard_map/ppermute | solution.py:32
  883.3 13.8 %collective-permute-start.30 = (f32[1,1024,128]{2,1,0:T(8,128)S(1)}, f32[1,1024,128]{2,1,0:T(8,128)S(1)}, u32[]{:S(2)}, u32[]{:S(2)}) collective-permute-start(f32[1,1024,128]{2,1,0:T(8,128)S(1)} %multiply_add_fusion.4), channel_id=1, source_target_pairs={{0,4},{4,8},{8,12},{12,16},{16,20},{20,24},{24,28},{28,32},{32,36}... | collective-permute-start | bytes 1572872 | tf_op jit(solution)/shard_map/ppermute | solution.py:32
  1000.1 14.6 %collective-permute-start.35 = (f32[1,1024,128]{2,1,0:T(8,128)S(1)}, f32[1,1024,128]{2,1,0:T(8,128)S(1)}, u32[]{:S(2)}, u32[]{:S(2)}) collective-permute-start(f32[1,1024,128]{2,1,0:T(8,128)S(1)} %broadcast_multiply_fusion.1), channel_id=1, source_target_pairs={{0,252},{4,0},{8,4},{12,8},{16,12},{20,16},{24,20},{28,24},{32,28}... | collective-permute-start | bytes 1572872 | tf_op jit(solution)/shard_map/ppermute | solution.py:32
  1092.6 13.8 %collective-permute-start.36 = (f32[1,1024,128]{2,1,0:T(8,128)S(1)}, f32[1,1024,128]{2,1,0:T(8,128)S(1)}, u32[]{:S(2)}, u32[]{:S(2)}) collective-permute-start(f32[1,1024,128]{2,1,0:T(8,128)S(1)} %multiply_add_fusion.2), channel_id=1, source_target_pairs={{0,4},{4,8},{8,12},{12,16},{16,20},{20,24},{24,28},{28,32},{32,36}... | collective-permute-start | bytes 1572872 | tf_op jit(solution)/shard_map/ppermute | solution.py:32
  1210.5 14.6 %collective-permute-start.41 = (f32[1,1024,128]{2,1,0:T(8,128)S(1)}, f32[1,1024,128]{2,1,0:T(8,128)S(1)}, u32[]{:S(2)}, u32[]{:S(2)}) collective-permute-start(f32[1,1024,128]{2,1,0:T(8,128)S(1)} %broadcast_multiply_fusion), channel_id=1, source_target_pairs={{0,252},{4,0},{8,4},{12,8},{16,12},{20,16},{24,20},{28,24},{32,28}... | collective-permute-start | bytes 1572872 | tf_op jit(solution)/shard_map/ppermute | solution.py:32
  (30 other events, 232.5 us)
where the time goes:
time: 1240 us; the launch traced here: 1230 us
  blocking collectives  866 us (70%)
  waiting for transfers between devices  205 us (17%)
  other arithmetic  79.4 us (6%)
  starting transfers between devices  62.8 us (5%)
    psum x11, blocking collectives, column_squares(): return lax.psum(jnp.sum(values * values, axis=(0, 1)), ('tm', 'site'))  866 us
    ppermute x14, waiting for transfers between devices, shifted(): return lax.ppermute(value, axis, pairs)  183 us
    add x56, other arithmetic, rotate_pair(): hyper_cos * former + hyper_sin * latter  45.8 us
    ppermute x14, starting transfers between devices, with_halo(): after = lax.ppermute(first, axis, down)  42.1 us
  transfers between devices with their start and end apart: 42, of which 30 were waited for; matrix products, arithmetic and copies ran while one was open for 0% of the time, Pallas kernels for 0%

commit v1 on v0

v1 whole, which is shorter than its diff:
```python
import math

import jax
import jax.numpy as jnp
from jax import lax
from jax.experimental import pallas as pl
from jax.experimental.pallas import tpu as pltpu
from jax.sharding import PartitionSpec as P

LX = 64
LY = 64
PANEL = 128
SLICES = 64
ITERS = 6

coupling = 0.7368
hop_angle = 0.125

AXES = ("tm", "site")
TIMES = 64
STRIPS = 4
HALF_ROWS = LY // 2
PAIRS = HALF_ROWS // 2
CORE_GROUPS = [
    [t * STRIPS + 2 * half + core for t in range(TIMES) for half in range(2)] for core in range(2)
]
CORE_SWAP = [(i, i ^ 1) for i in range(TIMES * STRIPS)]
VMEM_LIMIT = 50 * 1024 * 1024


def pack_kernel(initial_ref, fields_ref, out_ref):
    sign = jnp.where(lax.axis_index("tm") == 0, 1.0, -1.0).astype(jnp.float32)
    for q in range(8):
        rows = [
            initial_ref[pl.ds((2 * q + y) * LX + x, 8, stride=8), :]
            for y in range(2)
            for x in range(8)
        ]
        out_ref[pl.ds(q, PANEL, stride=16), :] = jnp.concatenate(rows, axis=0).T
        spin = fields_ref[:, q * 128 : (q + 1) * 128].astype(jnp.float32)
        growth = sign * jnp.exp(coupling * (2.0 * spin - 1.0))
        out_ref[pl.ds(8 + q, PANEL, stride=16), :] = jnp.broadcast_to(growth, (PANEL, 128))


def tables_kernel(bonds_ref, cos_ref, sin_ref, flat_ref):
    cos_less = math.cosh(hop_angle) - 1.0
    sin_full = math.sinh(hop_angle)
    upper = lax.broadcasted_iota(jnp.int32, (128, 128), 0) % 2 == 1
    for f in range(4):
        for q in range(8):
            low = bonds_ref[f : f + 1, q * 128 : (q + 1) * 128].astype(jnp.float32)
            high = bonds_ref[f : f + 1, 1024 + q * 128 : 1024 + (q + 1) * 128].astype(jnp.float32)
            both = jnp.where(
                upper, jnp.broadcast_to(high, (128, 128)), jnp.broadcast_to(low, (128, 128))
            )
            flat_ref[pl.ds(q * 128, 128), :] = both.T
        width = 4 if f < 2 else 8
        for i in range(128):
            start = (i // width) * width * 8 + i % width
            kept = flat_ref[pl.ds(start, 8, stride=width), :]
            cos_ref[f, i] = 1.0 + kept * cos_less
            sin_ref[f, i] = kept * sin_full


def rotate(former, latter, cos, sin):
    return cos * former + sin * latter, sin * former + cos * latter


def swap_halves(value, odd):
    return jnp.where(odd, pltpu.roll(value, 1, 1), pltpu.roll(value, 127, 1))


def solve_kernel(
    sites_ref, own_ref, other_ref, cos_ref, sin_ref, out_ref,
    flat, growth, direction, residual, image, answer, gradient, edge,
):
    core = lax.axis_index("site") % 2
    column = 2 * lax.axis_index("tm") + lax.axis_index("site") // 2
    odd = lax.broadcasted_iota(jnp.int32, (8, 128), 1) % 2 == 1

    for source_ref, place in ((own_ref, core), (other_ref, 1 - core)):
        for q in range(8):
            block = source_ref[pl.ds(q, PANEL, stride=16), :].T
            direction[pl.ds(place * 16 + 2 * q, 2)] = block.reshape(2, 8, 8, 128)
            block = source_ref[pl.ds(8 + q, PANEL, stride=16), :].T
            flat[pl.ds(place * 1024 + q * 128, 128), :] = block
    zero = jnp.zeros((8, 128), jnp.float32)
    for y in range(HALF_ROWS):
        for x in range(8):
            growth[y, x] = flat[pl.ds(y * LX + x, 8, stride=8), :]
            residual[y, x] = zero
            answer[y, x] = zero
            gradient[y, x] = zero

    site = sites_ref[column]
    source_lane = 2 * (column * SLICES // PANEL) + site // (HALF_ROWS * LX)
    source_x = site % LX
    here = (lax.broadcasted_iota(jnp.int32, (8, 128), 0) == source_x // 8) & (
        lax.broadcasted_iota(jnp.int32, (8, 128), 1) == source_lane
    )
    residual[(site // LX) % HALF_ROWS, source_x % 8] = jnp.where(here, 1.0, 0.0)

    def along_x(row, y):
        row = list(row)
        for j in range(4):
            i = y * 4 + j
            row[2 * j], row[2 * j + 1] = rotate(
                row[2 * j], row[2 * j + 1], cos_ref[0, i], sin_ref[0, i]
            )
        return row

    def along_x_shifted(row, y):
        row = list(row)
        for j in range(4):
            i = y * 4 + j
            cos, sin = cos_ref[1, i], sin_ref[1, i]
            if j < 3:
                row[2 * j + 1], row[2 * j + 2] = rotate(row[2 * j + 1], row[2 * j + 2], cos, sin)
            else:
                row[7], wrapped = rotate(row[7], pltpu.roll(row[0], 7, 0), cos, sin)
                row[0] = pltpu.roll(wrapped, 1, 0)
        return row

    def across(former, latter, family, pair):
        results = [
            rotate(former[x], latter[x], cos_ref[family, pair * 8 + x], sin_ref[family, pair * 8 + x])
            for x in range(8)
        ]
        return [r[0] for r in results], [r[1] for r in results]

    def across_halves(last, first):
        moved = [swap_halves(v, odd) for v in first]
        last, moved = across(last, moved, 3, PAIRS - 1)
        return last, [swap_halves(v, odd) for v in moved]

    def forward_pass(beta):
        def hopped(p):
            rows = []
            for y in (2 * p, 2 * p + 1):
                row = []
                for x in range(8):
                    value = gradient[y, x] + beta * direction[y, x]
                    direction[y, x] = value
                    row.append(pltpu.roll(value, 2, 1) * growth[y, x])
                rows.append(along_x_shifted(along_x(row, y), y))
            return across(rows[0], rows[1], 2, p)

        def put(row, y, total):
            for x in range(8):
                value = direction[y, x] + row[x]
                image[y, x] = value
                total = total + value * value
            return total

        first, last = hopped(0)
        for x in range(8):
            edge[x] = first[x]

        def step(p, carry):
            last, total = carry
            upper, lower = hopped(p)
            last, upper = across(last, upper, 3, p - 1)
            total = put(last, 2 * p - 1, total)
            total = put(upper, 2 * p, total)
            return lower, total

        last, total = lax.fori_loop(1, PAIRS, step, (last, zero))
        last, first = across_halves(last, [edge[x] for x in range(8)])
        total = put(last, HALF_ROWS - 1, total)
        total = put(first, 0, total)
        return jnp.sum(total, keepdims=True)

    def backward_pass(size):
        def updated(y):
            row = []
            for x in range(8):
                answer[y, x] = answer[y, x] + size * direction[y, x]
                value = residual[y, x] - size * image[y, x]
                residual[y, x] = value
                row.append(value)
            return row

        def finish(upper, lower, p, total):
            rows = across(upper, lower, 2, p)
            for row, y in zip(rows, (2 * p, 2 * p + 1)):
                row = along_x(along_x_shifted(row, y), y)
                for x in range(8):
                    value = residual[y, x] + pltpu.roll(row[x] * growth[y, x], 126, 1)
                    gradient[y, x] = value
                    total = total + value * value
            return total

        last, first = across_halves(updated(HALF_ROWS - 1), updated(0))
        for x in range(8):
            edge[x] = last[x]

        def step(p, carry):
            upper, total = carry
            lower, later = across(updated(2 * p + 1), updated(2 * p + 2), 3, p)
            total = finish(upper, lower, p, total)
            return later, total

        upper, total = lax.fori_loop(0, PAIRS - 1, step, (first, zero))
        total = finish(upper, [edge[x] for x in range(8)], PAIRS - 1, total)
        return jnp.sum(total, keepdims=True)

    def turn(k, carry):
        gamma, beta = carry
        squares = forward_pass(beta)
        size = jnp.where(k == 0, jnp.ones_like(gamma), gamma / squares)
        gamma_next = backward_pass(size)
        beta = jnp.where(k == 0, jnp.zeros_like(gamma), gamma_next / gamma)
        return gamma_next, beta

    one = jnp.ones((1, 1), jnp.float32)
    lax.fori_loop(0, ITERS + 1, turn, (one, one))

    for part, values in enumerate((answer, gradient)):
        for q in range(8):
            block = values[pl.ds(core * 16 + 2 * q, 2)].reshape(128, 128)
            out_ref[pl.ds(8 * part + q, PANEL, stride=16), :] = block.T


def unpack_kernel(arrived_ref, solution_ref, gradient_ref):
    for part, out_ref in enumerate((solution_ref, gradient_ref)):
        for q in range(8):
            block = arrived_ref[pl.ds(8 * part + q, PANEL, stride=16), :].T
            for y in range(2):
                for x in range(8):
                    i = y * 8 + x
                    out_ref[pl.ds((2 * q + y) * LX + x, 8, stride=8), :] = block[8 * i : 8 * i + 8]


def call(kernel, out_shape, scratch=(), smem_first=False, operands=1, cost=0):
    vmem = pl.BlockSpec(memory_space=pltpu.VMEM)
    in_specs = [vmem] * operands
    if smem_first:
        in_specs[0] = pl.BlockSpec(memory_space=pltpu.SMEM)
    return pl.pallas_call(
        kernel,
        out_shape=out_shape,
        in_specs=in_specs,
        out_specs=jax.tree.map(lambda _: vmem, out_shape),
        scratch_shapes=list(scratch),
        compiler_params=pltpu.CompilerParams(vmem_limit_bytes=VMEM_LIMIT),
        cost_estimate=pl.CostEstimate(flops=cost, bytes_accessed=1 << 20, transcendentals=0),
    )


def f32(*shape):
    return jax.ShapeDtypeStruct(shape, jnp.float32)


def exchange(values):
    parts = values.reshape(PANEL, 16, 128)
    moved = lax.all_to_all(parts, AXES, 0, 0, tiled=True, axis_index_groups=CORE_GROUPS)
    return moved.reshape(PANEL * 16, 128)


def body(fields, bonds, source_sites, initial):
    packed = call(pack_kernel, f32(PANEL * 16, 128), operands=2)(
        initial.reshape(1024, PANEL), fields
    )
    cos, sin = call(
        tables_kernel,
        (f32(4, 128, 8, 128), f32(4, 128, 8, 128)),
        scratch=[pltpu.VMEM((1024, 128), jnp.float32)],
        cost=10_000_000,
    )(bonds)
    own = exchange(packed)
    other = lax.ppermute(own, AXES, CORE_SWAP)
    lattice = pltpu.VMEM((HALF_ROWS, 8, 8, 128), jnp.float32)
    solved = call(
        solve_kernel,
        f32(PANEL * 16, 128),
        scratch=[pltpu.VMEM((2048, 128), jnp.float32)]
        + [lattice] * 6
        + [pltpu.VMEM((8, 8, 128), jnp.float32)],
        smem_first=True,
        operands=5,
    )(source_sites, own, other, cos, sin)
    arrived = exchange(solved)
    solution, gradient = call(unpack_kernel, (f32(1024, PANEL), f32(1024, PANEL)))(arrived)
    return solution.reshape(1, 1024, PANEL), gradient.reshape(1, 1024, PANEL)


def solution(mesh):
    placed = (P("tm", "site"), P(), P(), P("tm", "site", None))
    return jax.shard_map(
        body,
        mesh=mesh,
        in_specs=placed,
        out_specs=(P("tm", "site", None), P("tm", "site", None)),
        check_vma=False,
    )
```

time: 1240 us -> 126 us (0.10); the launches traced: 1230 us -> 125 us
  blocking collectives: 866 us -> 83.5 us
  waiting for transfers between devices: 205 us -> 0.01 us
  other arithmetic: 79.4 us -> 0 us
  starting transfers between devices: 62.8 us -> 0.01 us
  Pallas kernels: 0 us -> 38.1 us
    psum x11 -> x0, blocking collectives: 866 us -> none  [column_squares(): return lax.psum(jnp.sum(values * values, axis=(0, 1)), ('tm', 'site'))]
    ppermute x42 -> x1, waiting for transfers between devices: 205 us -> 0.01 us  [body(): other = lax.ppermute(own, AXES, CORE_SWAP)]
    all_to_all x0 -> x2, blocking collectives: none -> 83.5 us  [exchange(): lax.all_to_all(parts, AXES, 0, 0, tiled=True, axis_index_groups=CORE_GROUPS)]
    ppermute x42 -> x1, starting transfers between devices: 62.8 us -> 0.01 us  [body(): other = lax.ppermute(own, AXES, CORE_SWAP)]
    add x65 -> x0, other arithmetic: 49.2 us -> none  [the longest x56 45.8 us: rotate_pair(): hyper_cos * former + hyper_sin * latter]
    pallas_call x0 -> x4, Pallas kernels: none -> 38.1 us  [the longest x1 34.2 us: body(): call(solve_kernel, f32(PANEL * 16, 128), scratch=[pltpu.VMEM((2048, 128),...]
    another operation x56 -> x0, other arithmetic: 14.5 us -> none  [the longest x28 13.2 us: bond_pairs_x(): jnp.stack([former, latter], axis=3)]
  transfers between devices with their start and end apart: 42 -> 1, of which waited for: 30 -> 0; matrix products, arithmetic and copies ran while one was open for 0% -> 0% of each run, Pallas kernels for 0% -> 2%
where the time goes in v1:
time: 126 us; the launch traced here: 125 us
  blocking collectives  83.5 us (66%)
  Pallas kernels  38.1 us (30%)
  local copies, waits for them, and re-layouts  3.04 us (2%)
    all_to_all x2, blocking collectives, exchange(): lax.all_to_all(parts, AXES, 0, 0, tiled=True, axis_index_groups=CORE_GROUPS)  83.5 us
    pallas_call x1, Pallas kernels, body(): call(solve_kernel, f32(PANEL * 16, 128), scratch=[pltpu.VMEM((2048, 128),...  34.2 us
    unnamed x10, local copies, waits for them, and re-layouts  3.04 us
  transfers between devices with their start and end apart: 1, of which 0 were waited for; matrix products, arithmetic and copies ran while one was open for 0% of the time, Pallas kernels for 2%

profile of v1, /device:TPU:32, one launch (start us, length us, event | category | flops | bytes accessed | tf_op | source)
XLA Modules:
  0.0 125.3 jit_solution(1805737512971306621)
XLA Ops:
  0.6 0.0 copy-start.3
  0.6 0.0 copy-start.1
  0.7 1.0 copy-done.1
  1.7 0.0 copy-start.2
  1.7 0.7 copy-done.2
  2.4 0.0 copy-start.4
  2.4 0.5 shard_map.59
  2.9 45.5 %all_to_all.10 = f32[128,16,128]{2,1,0:T(8,128)S(1)} all-to-all(f32[128,16,128]{2,1,0:T(8,128)S(1)} %bitcast.8), channel_id=1, replica_groups={{0,2,4,6,8,10,12,14,16,18,20,22,24,26,28,30,32,34,36,38,40,42,44,46,48,..., dimensions={0} | all-to-all | bytes 2097152 | tf_op jit(solution)/shard_map/all_to_all | solution.py:256
  48.4 0.0 collective-permute-start
  48.4 0.0 copy-done.4
  48.4 2.1 %shard_map.60 = (f32[4,128,8,128]{3,2,1,0:T(8,128)S(1)}, f32[4,128,8,128]{3,2,1,0:T(8,128)}) custom-call(s32[4,2048]{1,0:T(4,128)S(1)} %copy-done.4), custom_call_target="tpu_custom_call" | custom-call | flops 10000000 | bytes 1048576 | tf_op jit(solution)/shard_map/pallas_call | solution.py:264
  50.5 0.0 copy-start
  50.5 1.3 %copy-done = f32[4,128,8,128]{3,2,1,0:T(8,128)} copy-done((f32[4,128,8,128]{3,2,1,0:T(8,128)}, f32[4,128,8,128]{3,2,1,0:T(8,128)S(1)}, u32[]{:S(2)}) %copy-start) | copy-done | bytes 2097176
  51.8 0.0 collective-permute-done.other_ref
  51.8 0.0 copy-done.3
  51.8 34.2 %shard_map.61 = f32[2048,128]{1,0:T(8,128)S(1)} custom-call(s32[128]{0:T(128)S(1)} %copy-done.3, f32[2048,128]{1,0:T(8,128)S(1)} %bitcast.10, f32[2048,128]{1,0:T(8,128)S(1)} %collective-permute-done.other_ref, f32[4,128,8,128]{3,2,1,0:T(8,128)} %copy-done, f32[4,128,8,128]{3,2,1,0:T(8,128)} %get-tuple-element.7.sin_ref), custom_call_target="tpu_custom_call" | custom-call | bytes 1048576 | tf_op jit(solution)/shard_map/pallas_call | solution.py:273
  86.0 37.9 %all_to_all.11 = f32[128,16,128]{2,1,0:T(8,128)S(1)} all-to-all(f32[128,16,128]{2,1,0:T(8,128)S(1)} %bitcast.11), channel_id=1, replica_groups={{0,2,4,6,8,10,12,14,16,18,20,22,24,26,28,30,32,34,36,38,40,42,44,46,48,..., dimensions={0} | all-to-all | bytes 2097152 | tf_op jit(solution)/shard_map/all_to_all | solution.py:256
  124.0 1.3 %shard_map.62 = (f32[1024,128]{1,0:T(8,128)}, f32[1024,128]{1,0:T(8,128)}) custom-call(f32[2048,128]{1,0:T(8,128)S(1)} %bitcast.7), custom_call_target="tpu_custom_call" | custom-call | bytes 1048576 | tf_op jit(solution)/shard_map/pallas_call | solution.py:283
Async XLA Ops:
  0.6 51.2 %copy-start.3 = (s32[128]{0:T(128)S(1)}, s32[128]{0:T(128)}, u32[]{:S(2)}) copy-start(s32[128]{0:T(128)} %sites_ref.1) | copy-start | bytes 1540
  0.6 1.0 copy-start.1
  1.7 0.7 copy-start.2
  2.4 46.0 %copy-start.4 = (s32[4,2048]{1,0:T(4,128)S(1)}, s32[4,2048]{1,0:T(4,128)}, u32[]{:S(2)}) copy-start(s32[4,2048]{1,0:T(4,128)} %bonds_ref.1) | copy-start | bytes 98308
  48.4 3.4 %collective-permute-start = (f32[2048,128]{1,0:T(8,128)S(1)}, f32[2048,128]{1,0:T(8,128)S(1)}, u32[]{:S(2)}, u32[]{:S(2)}) collective-permute-start(f32[2048,128]{1,0:T(8,128)S(1)} %bitcast.9), channel_id=1, source_target_pairs={{0,1},{1,0},{2,3},{3,2},{4,5},{5,4},{6,7},{7,6},{8,9},{9,8},{10,11... | collective-permute-start | bytes 3145736 | tf_op jit(solution)/shard_map/ppermute | solution.py:271
  50.5 1.3 %copy-start = (f32[4,128,8,128]{3,2,1,0:T(8,128)}, f32[4,128,8,128]{3,2,1,0:T(8,128)S(1)}, u32[]{:S(2)}) copy-start(f32[4,128,8,128]{3,2,1,0:T(8,128)S(1)} %get-tuple-element.6.cos_ref) | copy-start | bytes 6291460

commit v2 on v1

--- a/solution.py
+++ b/solution.py
@@ -164,7 +164,10 @@
             total = put(upper, 2 * p, total)
             return lower, total
 
-        last, total = lax.fori_loop(1, PAIRS, step, (last, zero))
+        carry = (last, zero)
+        for p in range(1, PAIRS):
+            carry = step(p, carry)
+        last, total = carry
         last, first = across_halves(last, [edge[x] for x in range(8)])
         total = put(last, HALF_ROWS - 1, total)
         total = put(first, 0, total)
@@ -200,7 +203,10 @@
             total = finish(upper, lower, p, total)
             return later, total
 
-        upper, total = lax.fori_loop(0, PAIRS - 1, step, (first, zero))
+        carry = (first, zero)
+        for p in range(PAIRS - 1):
+            carry = step(p, carry)
+        upper, total = carry
         total = finish(upper, [edge[x] for x in range(8)], PAIRS - 1, total)
         return jnp.sum(total, keepdims=True)
 
@@ -257,20 +263,15 @@
     return moved.reshape(PANEL * 16, 128)
 
 
-def body(fields, bonds, source_sites, initial):
-    packed = call(pack_kernel, f32(PANEL * 16, 128), operands=2)(
-        initial.reshape(1024, PANEL), fields
-    )
+def local_solve(source_sites, own, other, bonds):
     cos, sin = call(
         tables_kernel,
         (f32(4, 128, 8, 128), f32(4, 128, 8, 128)),
         scratch=[pltpu.VMEM((1024, 128), jnp.float32)],
         cost=10_000_000,
     )(bonds)
-    own = exchange(packed)
-    other = lax.ppermute(own, AXES, CORE_SWAP)
     lattice = pltpu.VMEM((HALF_ROWS, 8, 8, 128), jnp.float32)
-    solved = call(
+    return call(
         solve_kernel,
         f32(PANEL * 16, 128),
         scratch=[pltpu.VMEM((2048, 128), jnp.float32)]
@@ -279,6 +280,15 @@
         smem_first=True,
         operands=5,
     )(source_sites, own, other, cos, sin)
+
+
+def body(fields, bonds, source_sites, initial):
+    packed = call(pack_kernel, f32(PANEL * 16, 128), operands=2)(
+        initial.reshape(1024, PANEL), fields
+    )
+    own = exchange(packed)
+    other = lax.ppermute(own, AXES, CORE_SWAP)
+    solved = local_solve(source_sites, own, other, bonds)
     arrived = exchange(solved)
     solution, gradient = call(unpack_kernel, (f32(1024, PANEL), f32(1024, PANEL)))(arrived)
     return solution.reshape(1, 1024, PANEL), gradient.reshape(1, 1024, PANEL)

time: 126 us -> 109 us (0.87)
  Pallas kernels: 38.1 us -> 21.7 us
    pallas_call x2, Pallas kernels: 36.3 us -> 19.9 us  [the longest x1 17.8 us: local_solve(): call(solve_kernel, f32(PANEL * 16, 128), scratch=[pltpu.VMEM((2048, 128),...]
where the time goes in v2:
time: 109 us
  blocking collectives  83.5 us (77%)
  Pallas kernels  21.7 us (20%)
  local copies, waits for them, and re-layouts  3.04 us (3%)
    all_to_all x2, blocking collectives, exchange(): lax.all_to_all(parts, AXES, 0, 0, tiled=True, axis_index_groups=CORE_GROUPS)  83.5 us
    pallas_call x1, Pallas kernels, local_solve(): call(solve_kernel, f32(PANEL * 16, 128), scratch=[pltpu.VMEM((2048, 128),...  17.8 us
    unnamed x10, local copies, waits for them, and re-layouts  3.04 us
  transfers between devices with their start and end apart: 1, of which 0 were waited for; matrix products, arithmetic and copies ran while one was open for 0% of the time, Pallas kernels for 2%

profile of v2, /device:TPU:32, one launch (start us, length us, event | category | flops | bytes accessed | tf_op | source)
XLA Modules:
  0.0 108.9 jit_solution(2298280827743575316)
XLA Ops:
  0.6 0.0 copy-start.3
  0.6 0.0 copy-start.1
  0.7 1.0 copy-done.1
  1.7 0.0 copy-start.2
  1.7 0.7 copy-done.2
  2.4 0.0 copy-start.4
  2.4 0.5 shard_map.59
  2.9 45.5 %all_to_all.10 = f32[128,16,128]{2,1,0:T(8,128)S(1)} all-to-all(f32[128,16,128]{2,1,0:T(8,128)S(1)} %bitcast.8), channel_id=1, replica_groups={{0,2,4,6,8,10,12,14,16,18,20,22,24,26,28,30,32,34,36,38,40,42,44,46,48,..., dimensions={0} | all-to-all | bytes 2097152 | tf_op jit(solution)/shard_map/all_to_all | solution.py:262
  48.4 0.0 collective-permute-start
  48.4 0.0 copy-done.4
  48.4 2.1 %shard_map.60 = (f32[4,128,8,128]{3,2,1,0:T(8,128)S(1)}, f32[4,128,8,128]{3,2,1,0:T(8,128)}) custom-call(s32[4,2048]{1,0:T(4,128)S(1)} %copy-done.4), custom_call_target="tpu_custom_call" | custom-call | flops 10000000 | bytes 1048576 | tf_op jit(solution)/shard_map/pallas_call | solution.py:267
  50.5 0.0 copy-start
  50.5 1.3 %copy-done = f32[4,128,8,128]{3,2,1,0:T(8,128)} copy-done((f32[4,128,8,128]{3,2,1,0:T(8,128)}, f32[4,128,8,128]{3,2,1,0:T(8,128)S(1)}, u32[]{:S(2)}) %copy-start) | copy-done | bytes 2097176
  51.8 0.0 collective-permute-done.other_ref
  51.8 0.0 copy-done.3
  51.8 17.8 %shard_map.61 = f32[2048,128]{1,0:T(8,128)S(1)} custom-call(s32[128]{0:T(128)S(1)} %copy-done.3, f32[2048,128]{1,0:T(8,128)S(1)} %bitcast.10, f32[2048,128]{1,0:T(8,128)S(1)} %collective-permute-done.other_ref, f32[4,128,8,128]{3,2,1,0:T(8,128)} %copy-done, f32[4,128,8,128]{3,2,1,0:T(8,128)} %get-tuple-element.7.sin_ref), custom_call_target="tpu_custom_call" | custom-call | bytes 1048576 | tf_op jit(solution)/shard_map/pallas_call | solution.py:274
  69.6 37.9 %all_to_all.11 = f32[128,16,128]{2,1,0:T(8,128)S(1)} all-to-all(f32[128,16,128]{2,1,0:T(8,128)S(1)} %bitcast.11), channel_id=1, replica_groups={{0,2,4,6,8,10,12,14,16,18,20,22,24,26,28,30,32,34,36,38,40,42,44,46,48,..., dimensions={0} | all-to-all | bytes 2097152 | tf_op jit(solution)/shard_map/all_to_all | solution.py:262
  107.6 1.3 %shard_map.62 = (f32[1024,128]{1,0:T(8,128)}, f32[1024,128]{1,0:T(8,128)}) custom-call(f32[2048,128]{1,0:T(8,128)S(1)} %bitcast.7), custom_call_target="tpu_custom_call" | custom-call | bytes 1048576 | tf_op jit(solution)/shard_map/pallas_call | solution.py:293
Async XLA Ops:
  0.6 51.2 %copy-start.3 = (s32[128]{0:T(128)S(1)}, s32[128]{0:T(128)}, u32[]{:S(2)}) copy-start(s32[128]{0:T(128)} %sites_ref.1) | copy-start | bytes 1540
  0.6 1.0 copy-start.1
  1.7 0.7 copy-start.2
  2.4 46.0 %copy-start.4 = (s32[4,2048]{1,0:T(4,128)S(1)}, s32[4,2048]{1,0:T(4,128)}, u32[]{:S(2)}) copy-start(s32[4,2048]{1,0:T(4,128)} %bonds_ref.1) | copy-start | bytes 98308
  48.4 3.4 %collective-permute-start = (f32[2048,128]{1,0:T(8,128)S(1)}, f32[2048,128]{1,0:T(8,128)S(1)}, u32[]{:S(2)}, u32[]{:S(2)}) collective-permute-start(f32[2048,128]{1,0:T(8,128)S(1)} %bitcast.9), channel_id=1, source_target_pairs={{0,1},{1,0},{2,3},{3,2},{4,5},{5,4},{6,7},{7,6},{8,9},{9,8},{10,11... | collective-permute-start | bytes 3145736 | tf_op jit(solution)/shard_map/ppermute | solution.py:290
  50.5 1.3 %copy-start = (f32[4,128,8,128]{3,2,1,0:T(8,128)}, f32[4,128,8,128]{3,2,1,0:T(8,128)S(1)}, u32[]{:S(2)}) copy-start(f32[4,128,8,128]{3,2,1,0:T(8,128)S(1)} %get-tuple-element.6.cos_ref) | copy-start | bytes 6291460

commit v3 on v2

--- a/solution.py
+++ b/solution.py
@@ -25,6 +25,7 @@
     [t * STRIPS + 2 * half + core for t in range(TIMES) for half in range(2)] for core in range(2)
 ]
 CORE_SWAP = [(i, i ^ 1) for i in range(TIMES * STRIPS)]
+UNROLL = 15
 VMEM_LIMIT = 50 * 1024 * 1024
 
 
@@ -42,9 +43,10 @@
         out_ref[pl.ds(8 + q, PANEL, stride=16), :] = jnp.broadcast_to(growth, (PANEL, 128))
 
 
-def tables_kernel(bonds_ref, cos_ref, sin_ref, flat_ref):
+def tables_kernel(bonds_ref, tan_ref, mix_ref, flat_ref, cos_ref):
     cos_less = math.cosh(hop_angle) - 1.0
-    sin_full = math.sinh(hop_angle)
+    tangent = math.tanh(hop_angle)
+    odd = lax.broadcasted_iota(jnp.int32, (8, 128), 1) % 2 == 1
     upper = lax.broadcasted_iota(jnp.int32, (128, 128), 0) % 2 == 1
     for f in range(4):
         for q in range(8):
@@ -53,17 +55,40 @@
             both = jnp.where(
                 upper, jnp.broadcast_to(high, (128, 128)), jnp.broadcast_to(low, (128, 128))
             )
-            flat_ref[pl.ds(q * 128, 128), :] = both.T
+            flat_ref[f, pl.ds(q * 128, 128), :] = both.T
+        if f == 2:
+            continue
         width = 4 if f < 2 else 8
         for i in range(128):
             start = (i // width) * width * 8 + i % width
-            kept = flat_ref[pl.ds(start, 8, stride=width), :]
-            cos_ref[f, i] = 1.0 + kept * cos_less
-            sin_ref[f, i] = kept * sin_full
-
-
-def rotate(former, latter, cos, sin):
-    return cos * former + sin * latter, sin * former + cos * latter
+            kept = flat_ref[f, pl.ds(start, 8, stride=width), :]
+            tan_ref[f - f // 3, i] = kept * tangent
+            if f > 0:
+                cos_ref[f // 3, i] = 1.0 + kept * cos_less
+
+    def cos_along(y, x):
+        if x == 0:
+            return pltpu.roll(cos_ref[0, y * 4 + 3], 1, 0)
+        return cos_ref[0, y * 4 + (x - 1) // 2]
+
+    for p in range(PAIRS):
+        for x in range(8):
+            kept = flat_ref[2, pl.ds(p * 64 + x, 8, stride=8), :]
+            cos, sin = 1.0 + kept * cos_less, kept * math.sinh(hop_angle)
+            if p == 0:
+                before = swap_halves(cos_ref[1, (PAIRS - 1) * 8 + x], odd)
+            else:
+                before = cos_ref[1, (p - 1) * 8 + x]
+            after = cos_ref[1, p * 8 + x]
+            former, latter = cos_along(2 * p, x), cos_along(2 * p + 1, x)
+            mix_ref[0, p * 8 + x] = before * cos * former
+            mix_ref[1, p * 8 + x] = before * sin * latter
+            mix_ref[2, p * 8 + x] = after * sin * former
+            mix_ref[3, p * 8 + x] = after * cos * latter
+
+
+def join(former, latter, tan):
+    return former + tan * latter, latter + tan * former
 
 
 def swap_halves(value, odd):
@@ -71,7 +96,7 @@
 
 
 def solve_kernel(
-    sites_ref, own_ref, other_ref, cos_ref, sin_ref, out_ref,
+    sites_ref, own_ref, other_ref, tan_ref, mix_ref, out_ref,
     flat, growth, direction, residual, image, answer, gradient, edge,
 ):
     core = lax.axis_index("site") % 2
@@ -87,7 +112,8 @@
     zero = jnp.zeros((8, 128), jnp.float32)
     for y in range(HALF_ROWS):
         for x in range(8):
-            growth[y, x] = flat[pl.ds(y * LX + x, 8, stride=8), :]
+            cos = jnp.where(tan_ref[0, y * 4 + x // 2] > 0.0, math.cosh(hop_angle), 1.0)
+            growth[y, x] = flat[pl.ds(y * LX + x, 8, stride=8), :] * cos
             residual[y, x] = zero
             answer[y, x] = zero
             gradient[y, x] = zero
@@ -103,35 +129,53 @@
     def along_x(row, y):
         row = list(row)
         for j in range(4):
-            i = y * 4 + j
-            row[2 * j], row[2 * j + 1] = rotate(
-                row[2 * j], row[2 * j + 1], cos_ref[0, i], sin_ref[0, i]
-            )
+            row[2 * j], row[2 * j + 1] = join(row[2 * j], row[2 * j + 1], tan_ref[0, y * 4 + j])
         return row
 
     def along_x_shifted(row, y):
         row = list(row)
-        for j in range(4):
-            i = y * 4 + j
-            cos, sin = cos_ref[1, i], sin_ref[1, i]
-            if j < 3:
-                row[2 * j + 1], row[2 * j + 2] = rotate(row[2 * j + 1], row[2 * j + 2], cos, sin)
-            else:
-                row[7], wrapped = rotate(row[7], pltpu.roll(row[0], 7, 0), cos, sin)
-                row[0] = pltpu.roll(wrapped, 1, 0)
+        for j in range(3):
+            row[2 * j + 1], row[2 * j + 2] = join(
+                row[2 * j + 1], row[2 * j + 2], tan_ref[1, y * 4 + j]
+            )
+        row[7], wrapped = join(row[7], pltpu.roll(row[0], 7, 0), tan_ref[1, y * 4 + 3])
+        row[0] = pltpu.roll(wrapped, 1, 0)
         return row
 
-    def across(former, latter, family, pair):
-        results = [
-            rotate(former[x], latter[x], cos_ref[family, pair * 8 + x], sin_ref[family, pair * 8 + x])
-            for x in range(8)
-        ]
+    def mixed(former, latter, pair, order):
+        results = [[], []]
+        for x in range(8):
+            i = pair * 8 + x
+            for side, (m, n) in enumerate(order):
+                results[side].append(mix_ref[m, i] * former[x] + mix_ref[n, i] * latter[x])
+        return results
+
+    def across(former, latter, pair):
+        results = [join(former[x], latter[x], tan_ref[2, pair * 8 + x]) for x in range(8)]
         return [r[0] for r in results], [r[1] for r in results]
 
     def across_halves(last, first):
         moved = [swap_halves(v, odd) for v in first]
-        last, moved = across(last, moved, 3, PAIRS - 1)
+        last, moved = across(last, moved, PAIRS - 1)
         return last, [swap_halves(v, odd) for v in moved]
+
+    def add_squares(totals, x, value):
+        totals = list(totals)
+        totals[x % 4] = totals[x % 4] + value * value
+        return totals
+
+    def loop(first, steps, step, carry):
+        if steps % UNROLL:
+            raise ValueError("bad unroll")
+
+        def turn(i, carry):
+            for j in range(UNROLL):
+                carry = step(first + i * UNROLL + j, carry)
+            return carry
+
+        if steps == UNROLL:
+            return turn(0, carry)
+        return lax.fori_loop(0, steps // UNROLL, turn, carry)
 
     def forward_pass(beta):
         def hopped(p):
@@ -143,35 +187,32 @@
                     direction[y, x] = value
                     row.append(pltpu.roll(value, 2, 1) * growth[y, x])
                 rows.append(along_x_shifted(along_x(row, y), y))
-            return across(rows[0], rows[1], 2, p)
-
-        def put(row, y, total):
+            return mixed(rows[0], rows[1], p, ((0, 1), (2, 3)))
+
+        def put(row, y, totals):
             for x in range(8):
                 value = direction[y, x] + row[x]
                 image[y, x] = value
-                total = total + value * value
-            return total
+                totals = add_squares(totals, x, value)
+            return totals
 
         first, last = hopped(0)
         for x in range(8):
             edge[x] = first[x]
 
         def step(p, carry):
-            last, total = carry
+            last, totals = carry
             upper, lower = hopped(p)
-            last, upper = across(last, upper, 3, p - 1)
-            total = put(last, 2 * p - 1, total)
-            total = put(upper, 2 * p, total)
-            return lower, total
-
-        carry = (last, zero)
-        for p in range(1, PAIRS):
-            carry = step(p, carry)
-        last, total = carry
+            last, upper = across(last, upper, p - 1)
+            totals = put(last, 2 * p - 1, totals)
+            totals = put(upper, 2 * p, totals)
+            return lower, totals
+
+        last, totals = loop(1, PAIRS - 1, step, (last, [zero] * 4))
         last, first = across_halves(last, [edge[x] for x in range(8)])
-        total = put(last, HALF_ROWS - 1, total)
-        total = put(first, 0, total)
-        return jnp.sum(total, keepdims=True)
+        totals = put(last, HALF_ROWS - 1, totals)
+        totals = put(first, 0, totals)
+        return jnp.sum(sum(totals), keepdims=True)
 
     def backward_pass(size):
         def updated(y):
@@ -183,32 +224,29 @@
                 row.append(value)
             return row
 
-        def finish(upper, lower, p, total):
-            rows = across(upper, lower, 2, p)
+        def finish(upper, lower, p, totals):
+            rows = mixed(upper, lower, p, ((0, 2), (1, 3)))
             for row, y in zip(rows, (2 * p, 2 * p + 1)):
                 row = along_x(along_x_shifted(row, y), y)
                 for x in range(8):
                     value = residual[y, x] + pltpu.roll(row[x] * growth[y, x], 126, 1)
                     gradient[y, x] = value
-                    total = total + value * value
-            return total
+                    totals = add_squares(totals, x, value)
+            return totals
 
         last, first = across_halves(updated(HALF_ROWS - 1), updated(0))
         for x in range(8):
             edge[x] = last[x]
 
         def step(p, carry):
-            upper, total = carry
-            lower, later = across(updated(2 * p + 1), updated(2 * p + 2), 3, p)
-            total = finish(upper, lower, p, total)
-            return later, total
-
-        carry = (first, zero)
-        for p in range(PAIRS - 1):
-            carry = step(p, carry)
-        upper, total = carry
-        total = finish(upper, [edge[x] for x in range(8)], PAIRS - 1, total)
-        return jnp.sum(total, keepdims=True)
+            upper, totals = carry
+            lower, later = across(updated(2 * p + 1), updated(2 * p + 2), p)
+            totals = finish(upper, lower, p, totals)
+            return later, totals
+
+        upper, totals = loop(0, PAIRS - 1, step, (first, [zero] * 4))
+        totals = finish(upper, [edge[x] for x in range(8)], PAIRS - 1, totals)
+        return jnp.sum(sum(totals), keepdims=True)
 
     def turn(k, carry):
         gamma, beta = carry
@@ -264,10 +302,13 @@
 
 
 def local_solve(source_sites, own, other, bonds):
-    cos, sin = call(
+    tan, mix = call(
         tables_kernel,
-        (f32(4, 128, 8, 128), f32(4, 128, 8, 128)),
-        scratch=[pltpu.VMEM((1024, 128), jnp.float32)],
+        (f32(3, 128, 8, 128), f32(4, 128, 8, 128)),
+        scratch=[
+            pltpu.VMEM((4, 1024, 128), jnp.float32),
+            pltpu.VMEM((2, 128, 8, 128), jnp.float32),
+        ],
         cost=10_000_000,
     )(bonds)
     lattice = pltpu.VMEM((HALF_ROWS, 8, 8, 128), jnp.float32)
@@ -279,7 +320,7 @@
         + [pltpu.VMEM((8, 8, 128), jnp.float32)],
         smem_first=True,
         operands=5,
-    )(source_sites, own, other, cos, sin)
+    )(source_sites, own, other, tan, mix)
 
 
 def body(fields, bonds, source_sites, initial):

time: 109 us -> 107 us (0.982)
  Pallas kernels: 21.7 us -> 18.4 us
  local copies, waits for them, and re-layouts: 3.04 us -> 4.21 us
    pallas_call x1, Pallas kernels: 17.8 us -> 15.6 us  [local_solve(): call(solve_kernel, f32(PANEL * 16, 128), scratch=[pltpu.VMEM((2048, 128),...]
    unnamed x10 -> x12, local copies, waits for them, and re-layouts: 3.04 us -> 4.21 us
    pallas_call x1, Pallas kernels: 2.1 us -> 0.96 us  [local_solve(): call(tables_kernel, (f32(3, 128, 8, 128), f32(4, 128, 8, 128)), scratch=[...]
  transfers between devices with their start and end apart: 1 -> 1, of which waited for: 0 -> 0; matrix products, arithmetic and copies ran while one was open for 0% -> 0% of each run, Pallas kernels for 2% -> 1%
where the time goes in v3:
time: 107 us
  blocking collectives  83.5 us (78%)
  Pallas kernels  18.4 us (17%)
  local copies, waits for them, and re-layouts  4.21 us (4%)
    all_to_all x2, blocking collectives, exchange(): lax.all_to_all(parts, AXES, 0, 0, tiled=True, axis_index_groups=CORE_GROUPS)  83.5 us
    pallas_call x1, Pallas kernels, local_solve(): call(solve_kernel, f32(PANEL * 16, 128), scratch=[pltpu.VMEM((2048, 128),...  15.6 us
    unnamed x12, local copies, waits for them, and re-layouts  4.21 us
  transfers between devices with their start and end apart: 1, of which 0 were waited for; matrix products, arithmetic and copies ran while one was open for 0% of the time, Pallas kernels for 1%

profile of v3, /device:TPU:32, one launch (start us, length us, event | category | flops | bytes accessed | tf_op | source)
XLA Modules:
  0.0 106.7 jit_solution(10675908121412573090)
XLA Ops:
  0.6 0.0 copy-start.4
  0.6 0.0 copy-start.2
  0.7 1.0 copy-done.2
  1.7 0.0 copy-start.3
  1.7 0.7 copy-done.3
  2.4 0.0 copy-start.5
  2.4 0.5 shard_map.59
  2.9 45.5 %all_to_all.10 = f32[128,16,128]{2,1,0:T(8,128)S(1)} all-to-all(f32[128,16,128]{2,1,0:T(8,128)S(1)} %bitcast.8), channel_id=1, replica_groups={{0,2,4,6,8,10,12,14,16,18,20,22,24,26,28,30,32,34,36,38,40,42,44,46,48,..., dimensions={0} | all-to-all | bytes 2097152 | tf_op jit(solution)/shard_map/all_to_all | solution.py:300
  48.4 0.0 collective-permute-start
  48.4 0.0 copy-done.5
  48.4 1.0 shard_map.60
  49.4 0.0 copy-start
  49.4 1.3 %copy-done = f32[4,128,8,128]{3,2,1,0:T(8,128)} copy-done((f32[4,128,8,128]{3,2,1,0:T(8,128)}, f32[4,128,8,128]{3,2,1,0:T(8,128)S(1)}, u32[]{:S(2)}) %copy-start) | copy-done | bytes 2097176
  50.7 0.0 copy-start.1
  50.7 1.1 %copy-done.1 = f32[3,128,8,128]{3,2,1,0:T(8,128)} copy-done((f32[3,128,8,128]{3,2,1,0:T(8,128)}, f32[3,128,8,128]{3,2,1,0:T(8,128)S(1)}, u32[]{:S(2)}) %copy-start.1) | copy-done | bytes 1572888
  51.9 0.0 collective-permute-done.other_ref
  51.9 0.0 copy-done.4
  51.9 15.6 %shard_map.61 = f32[2048,128]{1,0:T(8,128)S(1)} custom-call(s32[128]{0:T(128)S(1)} %copy-done.4, f32[2048,128]{1,0:T(8,128)S(1)} %bitcast.10, f32[2048,128]{1,0:T(8,128)S(1)} %collective-permute-done.other_ref, f32[3,128,8,128]{3,2,1,0:T(8,128)} %copy-done.1, f32[4,128,8,128]{3,2,1,0:T(8,128)} %copy-done), custom_call_target="tpu_custom_call" | custom-call | bytes 1048576 | tf_op jit(solution)/shard_map/pallas_call | solution.py:315
  67.5 37.9 %all_to_all.11 = f32[128,16,128]{2,1,0:T(8,128)S(1)} all-to-all(f32[128,16,128]{2,1,0:T(8,128)S(1)} %bitcast.11), channel_id=1, replica_groups={{0,2,4,6,8,10,12,14,16,18,20,22,24,26,28,30,32,34,36,38,40,42,44,46,48,..., dimensions={0} | all-to-all | bytes 2097152 | tf_op jit(solution)/shard_map/all_to_all | solution.py:300
  105.4 1.3 %shard_map.62 = (f32[1024,128]{1,0:T(8,128)}, f32[1024,128]{1,0:T(8,128)}) custom-call(f32[2048,128]{1,0:T(8,128)S(1)} %bitcast.7), custom_call_target="tpu_custom_call" | custom-call | bytes 1048576 | tf_op jit(solution)/shard_map/pallas_call | solution.py:334
Async XLA Ops:
  0.6 51.3 %copy-start.4 = (s32[128]{0:T(128)S(1)}, s32[128]{0:T(128)}, u32[]{:S(2)}) copy-start(s32[128]{0:T(128)} %sites_ref.1) | copy-start | bytes 1540
  0.6 1.0 copy-start.2
  1.7 0.7 copy-start.3
  2.4 46.0 %copy-start.5 = (s32[4,2048]{1,0:T(4,128)S(1)}, s32[4,2048]{1,0:T(4,128)}, u32[]{:S(2)}) copy-start(s32[4,2048]{1,0:T(4,128)} %bonds_ref.1) | copy-start | bytes 98308
  48.4 3.5 %collective-permute-start = (f32[2048,128]{1,0:T(8,128)S(1)}, f32[2048,128]{1,0:T(8,128)S(1)}, u32[]{:S(2)}, u32[]{:S(2)}) collective-permute-start(f32[2048,128]{1,0:T(8,128)S(1)} %bitcast.9), channel_id=1, source_target_pairs={{0,1},{1,0},{2,3},{3,2},{4,5},{5,4},{6,7},{7,6},{8,9},{9,8},{10,11... | collective-permute-start | bytes 3145736 | tf_op jit(solution)/shard_map/ppermute | solution.py:331
  49.4 1.3 %copy-start = (f32[4,128,8,128]{3,2,1,0:T(8,128)}, f32[4,128,8,128]{3,2,1,0:T(8,128)S(1)}, u32[]{:S(2)}) copy-start(f32[4,128,8,128]{3,2,1,0:T(8,128)S(1)} %get-tuple-element.7.mix_ref) | copy-start | bytes 6291460
  50.7 1.1 %copy-start.1 = (f32[3,128,8,128]{3,2,1,0:T(8,128)}, f32[3,128,8,128]{3,2,1,0:T(8,128)S(1)}, u32[]{:S(2)}) copy-start(f32[3,128,8,128]{3,2,1,0:T(8,128)S(1)} %get-tuple-element.6.tan_ref) | copy-start | bytes 4718596

commit v4 on v3

--- a/solution.py
+++ b/solution.py
@@ -25,8 +25,7 @@
     [t * STRIPS + 2 * half + core for t in range(TIMES) for half in range(2)] for core in range(2)
 ]
 CORE_SWAP = [(i, i ^ 1) for i in range(TIMES * STRIPS)]
-UNROLL = 15
-VMEM_LIMIT = 50 * 1024 * 1024
+VMEM_LIMIT = 24 * 1024 * 1024
 
 
 def pack_kernel(initial_ref, fields_ref, out_ref):
@@ -97,7 +96,7 @@
 
 def solve_kernel(
     sites_ref, own_ref, other_ref, tan_ref, mix_ref, out_ref,
-    flat, growth, direction, residual, image, answer, gradient, edge,
+    flat, growth, growth_before, gradient, history, image, edge, steps, betas,
 ):
     core = lax.axis_index("site") % 2
     column = 2 * lax.axis_index("tm") + lax.axis_index("site") // 2
@@ -106,17 +105,18 @@
     for source_ref, place in ((own_ref, core), (other_ref, 1 - core)):
         for q in range(8):
             block = source_ref[pl.ds(q, PANEL, stride=16), :].T
-            direction[pl.ds(place * 16 + 2 * q, 2)] = block.reshape(2, 8, 8, 128)
+            gradient[pl.ds(place * 16 + 2 * q, 2)] = block.reshape(2, 8, 8, 128)
             block = source_ref[pl.ds(8 + q, PANEL, stride=16), :].T
             flat[pl.ds(place * 1024 + q * 128, 128), :] = block
     zero = jnp.zeros((8, 128), jnp.float32)
     for y in range(HALF_ROWS):
         for x in range(8):
             cos = jnp.where(tan_ref[0, y * 4 + x // 2] > 0.0, math.cosh(hop_angle), 1.0)
-            growth[y, x] = flat[pl.ds(y * LX + x, 8, stride=8), :] * cos
-            residual[y, x] = zero
-            answer[y, x] = zero
-            gradient[y, x] = zero
+            value = flat[pl.ds(y * LX + x, 8, stride=8), :] * cos
+            growth[y, x] = value
+            growth_before[y, x] = pltpu.roll(value, 126, 1)
+            image[y, x] = zero
+            history[ITERS + 1, y, x] = zero
 
     site = sites_ref[column]
     source_lane = 2 * (column * SLICES // PANEL) + site // (HALF_ROWS * LX)
@@ -124,7 +124,7 @@
     here = (lax.broadcasted_iota(jnp.int32, (8, 128), 0) == source_x // 8) & (
         lax.broadcasted_iota(jnp.int32, (8, 128), 1) == source_lane
     )
-    residual[(site // LX) % HALF_ROWS, source_x % 8] = jnp.where(here, 1.0, 0.0)
+    image[(site // LX) % HALF_ROWS, source_x % 8] = jnp.where(here, 1.0, 0.0)
 
     def along_x(row, y):
         row = list(row)
@@ -164,105 +164,93 @@
         totals[x % 4] = totals[x % 4] + value * value
         return totals
 
-    def loop(first, steps, step, carry):
-        if steps % UNROLL:
-            raise ValueError("bad unroll")
-
-        def turn(i, carry):
-            for j in range(UNROLL):
-                carry = step(first + i * UNROLL + j, carry)
-            return carry
-
-        if steps == UNROLL:
-            return turn(0, carry)
-        return lax.fori_loop(0, steps // UNROLL, turn, carry)
-
-    def forward_pass(beta):
+    def forward_pass(k, beta):
         def hopped(p):
             rows = []
             for y in (2 * p, 2 * p + 1):
                 row = []
                 for x in range(8):
-                    value = gradient[y, x] + beta * direction[y, x]
-                    direction[y, x] = value
-                    row.append(pltpu.roll(value, 2, 1) * growth[y, x])
+                    value = gradient[y, x]
+                    history[k, y, x] = value
+                    row.append(value * growth_before[y, x])
                 rows.append(along_x_shifted(along_x(row, y), y))
             return mixed(rows[0], rows[1], p, ((0, 1), (2, 3)))
 
         def put(row, y, totals):
             for x in range(8):
-                value = direction[y, x] + row[x]
+                value = (gradient[y, x] + pltpu.roll(row[x], 2, 1)) + beta * image[y, x]
                 image[y, x] = value
                 totals = add_squares(totals, x, value)
             return totals
 
+        totals = [zero] * 4
         first, last = hopped(0)
         for x in range(8):
             edge[x] = first[x]
-
-        def step(p, carry):
-            last, totals = carry
+        for p in range(1, PAIRS):
             upper, lower = hopped(p)
             last, upper = across(last, upper, p - 1)
             totals = put(last, 2 * p - 1, totals)
             totals = put(upper, 2 * p, totals)
-            return lower, totals
-
-        last, totals = loop(1, PAIRS - 1, step, (last, [zero] * 4))
+            last = lower
         last, first = across_halves(last, [edge[x] for x in range(8)])
         totals = put(last, HALF_ROWS - 1, totals)
-        totals = put(first, 0, totals)
-        return jnp.sum(sum(totals), keepdims=True)
-
-    def backward_pass(size):
-        def updated(y):
-            row = []
-            for x in range(8):
-                answer[y, x] = answer[y, x] + size * direction[y, x]
-                value = residual[y, x] - size * image[y, x]
-                residual[y, x] = value
-                row.append(value)
-            return row
+        return put(first, 0, totals)
+
+    def backward_pass(base, size):
+        def loaded(y):
+            return [image[y, x] for x in range(8)]
 
         def finish(upper, lower, p, totals):
             rows = mixed(upper, lower, p, ((0, 2), (1, 3)))
             for row, y in zip(rows, (2 * p, 2 * p + 1)):
                 row = along_x(along_x_shifted(row, y), y)
                 for x in range(8):
-                    value = residual[y, x] + pltpu.roll(row[x] * growth[y, x], 126, 1)
+                    value = image[y, x] + pltpu.roll(row[x] * growth[y, x], 126, 1)
+                    value = history[base, y, x] - size * value
                     gradient[y, x] = value
                     totals = add_squares(totals, x, value)
             return totals
 
-        last, first = across_halves(updated(HALF_ROWS - 1), updated(0))
+        totals = [zero] * 4
+        last, upper = across_halves(loaded(HALF_ROWS - 1), loaded(0))
         for x in range(8):
             edge[x] = last[x]
-
-        def step(p, carry):
-            upper, totals = carry
-            lower, later = across(updated(2 * p + 1), updated(2 * p + 2), p)
+        for p in range(PAIRS - 1):
+            lower, later = across(loaded(2 * p + 1), loaded(2 * p + 2), p)
             totals = finish(upper, lower, p, totals)
-            return later, totals
-
-        upper, totals = loop(0, PAIRS - 1, step, (first, [zero] * 4))
-        totals = finish(upper, [edge[x] for x in range(8)], PAIRS - 1, totals)
+            upper = later
+        return finish(upper, [edge[x] for x in range(8)], PAIRS - 1, totals)
+
+    def whole(totals):
         return jnp.sum(sum(totals), keepdims=True)
 
     def turn(k, carry):
-        gamma, beta = carry
-        squares = forward_pass(beta)
-        size = jnp.where(k == 0, jnp.ones_like(gamma), gamma / squares)
-        gamma_next = backward_pass(size)
-        beta = jnp.where(k == 0, jnp.zeros_like(gamma), gamma_next / gamma)
-        return gamma_next, beta
-
-    one = jnp.ones((1, 1), jnp.float32)
-    lax.fori_loop(0, ITERS + 1, turn, (one, one))
-
-    for part, values in enumerate((answer, gradient)):
-        for q in range(8):
-            block = values[pl.ds(core * 16 + 2 * q, 2)].reshape(128, 128)
-            out_ref[pl.ds(8 * part + q, PANEL, stride=16), :] = block.T
+        gamma_before, totals = carry
+        gamma = whole(totals)
+        beta = jnp.where(k < 2, 0.0, gamma / gamma_before)
+        beta = jnp.where(k == 0, -1.0, beta)
+        squares = whole(forward_pass(k, beta))
+        size = jnp.where(k == 0, 1.0, gamma / squares)
+        betas[k] = jnp.broadcast_to(beta, (8, 128))
+        steps[k] = jnp.broadcast_to(size, (8, 128))
+        base = jnp.where(k == 0, ITERS + 1, k)
+        return gamma, backward_pass(base, size)
+
+    one = jnp.ones((8, 128), jnp.float32)
+    lax.fori_loop(0, ITERS + 1, turn, (jnp.ones((1, 1), jnp.float32), [one] * 4))
+
+    weights = [steps[ITERS]]
+    for k in range(ITERS - 1, 0, -1):
+        weights.insert(0, steps[k] + betas[k + 1] * weights[0])
+    for q in range(8):
+        mine = pl.ds(core * 16 + 2 * q, 2)
+        total = history[0, mine]
+        for k in range(1, ITERS + 1):
+            total = total + weights[k - 1] * history[k, mine]
+        out_ref[pl.ds(q, PANEL, stride=16), :] = total.reshape(128, 128).T
+        block = gradient[mine].reshape(128, 128)
+        out_ref[pl.ds(8 + q, PANEL, stride=16), :] = block.T
 
 
 def unpack_kernel(arrived_ref, solution_ref, gradient_ref):
@@ -316,8 +304,10 @@
         solve_kernel,
         f32(PANEL * 16, 128),
         scratch=[pltpu.VMEM((2048, 128), jnp.float32)]
-        + [lattice] * 6
-        + [pltpu.VMEM((8, 8, 128), jnp.float32)],
+        + [lattice] * 3
+        + [pltpu.VMEM((ITERS + 2, HALF_ROWS, 8, 8, 128), jnp.float32)]
+        + [lattice]
+        + [pltpu.VMEM((8, 8, 128), jnp.float32)] * 3,
         smem_first=True,
         operands=5,
     )(source_sites, own, other, tan, mix)

time: 107 us -> 103 us (0.963)
  Pallas kernels: 18.4 us -> 15.2 us
  local copies, waits for them, and re-layouts: 4.21 us -> 1.73 us
  waiting for transfers between devices: 0.01 us -> 1.68 us
    pallas_call x1, Pallas kernels: 15.6 us -> 12.4 us  [local_solve(): call(solve_kernel, f32(PANEL * 16, 128), scratch=[pltpu.VMEM((2048, 128),...]
    unnamed x12 -> x8, local copies, waits for them, and re-layouts: 4.21 us -> 1.73 us
    ppermute x1, waiting for transfers between devices: 0.01 us -> 1.68 us  [body(): other = lax.ppermute(own, AXES, CORE_SWAP)]
  transfers between devices with their start and end apart: 1 -> 1, of which waited for: 0 -> 1; matrix products, arithmetic and copies ran while one was open for 0% -> 0% of each run, Pallas kernels for 1% -> 1%
where the time goes in v4:
time: 103 us; the launch traced here: 102 us
  blocking collectives  83.1 us (81%)
  Pallas kernels  15.2 us (15%)
  local copies, waits for them, and re-layouts  1.73 us (2%)
  waiting for transfers between devices  1.68 us (2%)
    all_to_all x2, blocking collectives, exchange(): lax.all_to_all(parts, AXES, 0, 0, tiled=True, axis_index_groups=CORE_GROUPS)  83.1 us
    pallas_call x1, Pallas kernels, local_solve(): call(solve_kernel, f32(PANEL * 16, 128), scratch=[pltpu.VMEM((2048, 128),...  12.4 us
  transfers between devices with their start and end apart: 1, of which 1 were waited for; matrix products, arithmetic and copies ran while one was open for 0% of the time, Pallas kernels for 1%

profile of v4, /device:TPU:32, one launch (start us, length us, event | category | flops | bytes accessed | tf_op | source)
XLA Modules:
  0.0 102.4 jit_solution(8957112914764865265)
XLA Ops:
  0.6 0.0 copy-start.2
  0.6 0.0 copy-start
  0.7 1.0 %copy-done = f32[1,1024,128]{2,1,0:T(8,128)S(1)} copy-done((f32[1,1024,128]{2,1,0:T(8,128)S(1)}, f32[1,1024,128]{2,1,0:T(8,128)}, u32[]{:S(2)}) %copy-start) | copy-done | bytes 524312
  1.7 0.0 copy-start.1
  1.7 0.7 copy-done.1
  2.4 0.0 copy-start.3
  2.4 0.5 shard_map.59
  2.9 45.5 %all_to_all.10 = f32[128,16,128]{2,1,0:T(8,128)S(1)} all-to-all(f32[128,16,128]{2,1,0:T(8,128)S(1)} %bitcast.8), channel_id=1, replica_groups={{0,2,4,6,8,10,12,14,16,18,20,22,24,26,28,30,32,34,36,38,40,42,44,46,48,..., dimensions={0} | all-to-all | bytes 2097152 | tf_op jit(solution)/shard_map/all_to_all | solution.py:288
  48.4 0.0 collective-permute-start
  48.4 0.0 copy-done.3
  48.4 1.0 shard_map.60
  49.4 1.7 %collective-permute-done.other_ref = f32[2048,128]{1,0:T(8,128)S(1)} collective-permute-done((f32[2048,128]{1,0:T(8,128)S(1)}, f32[2048,128]{1,0:T(8,128)S(1)}, u32[]{:S(2)}, u32[]{:S(2)}) %collective-permute-start) | collective-permute-done | bytes 1048608 | tf_op jit(solution)/shard_map/ppermute | solution.py:321
  51.1 0.0 copy-done.2
  51.1 12.4 %shard_map.61 = f32[2048,128]{1,0:T(8,128)S(1)} custom-call(s32[128]{0:T(128)S(1)} %copy-done.2, f32[2048,128]{1,0:T(8,128)S(1)} %bitcast.10, f32[2048,128]{1,0:T(8,128)S(1)} %collective-permute-done.other_ref, f32[3,128,8,128]{3,2,1,0:T(8,128)S(1)} %get-tuple-element.6.tan_ref, f32[4,128,8,128]{3,2,1,0:T(8,128)S(1)} %get-tuple-element.7.mix_ref), custom_call_target="tpu_custom_call" | custom-call | bytes 1048576 | tf_op jit(solution)/shard_map/pallas_call | solution.py:303
  63.5 37.6 %all_to_all.11 = f32[128,16,128]{2,1,0:T(8,128)S(1)} all-to-all(f32[128,16,128]{2,1,0:T(8,128)S(1)} %bitcast.11), channel_id=1, replica_groups={{0,2,4,6,8,10,12,14,16,18,20,22,24,26,28,30,32,34,36,38,40,42,44,46,48,..., dimensions={0} | all-to-all | bytes 2097152 | tf_op jit(solution)/shard_map/all_to_all | solution.py:288
  101.0 1.3 %shard_map.62 = (f32[1024,128]{1,0:T(8,128)}, f32[1024,128]{1,0:T(8,128)}) custom-call(f32[2048,128]{1,0:T(8,128)S(1)} %bitcast.7), custom_call_target="tpu_custom_call" | custom-call | bytes 1048576 | tf_op jit(solution)/shard_map/pallas_call | solution.py:324
Async XLA Ops:
  0.6 50.4 %copy-start.2 = (s32[128]{0:T(128)S(1)}, s32[128]{0:T(128)}, u32[]{:S(2)}) copy-start(s32[128]{0:T(128)} %sites_ref.1) | copy-start | bytes 1540
  0.6 1.0 %copy-start = (f32[1,1024,128]{2,1,0:T(8,128)S(1)}, f32[1,1024,128]{2,1,0:T(8,128)}, u32[]{:S(2)}) copy-start(f32[1,1024,128]{2,1,0:T(8,128)} %param.7) | copy-start | bytes 1572868
  1.7 0.7 copy-start.1
  2.4 46.0 %copy-start.3 = (s32[4,2048]{1,0:T(4,128)S(1)}, s32[4,2048]{1,0:T(4,128)}, u32[]{:S(2)}) copy-start(s32[4,2048]{1,0:T(4,128)} %bonds_ref.1) | copy-start | bytes 98308
  48.4 2.7 %collective-permute-start = (f32[2048,128]{1,0:T(8,128)S(1)}, f32[2048,128]{1,0:T(8,128)S(1)}, u32[]{:S(2)}, u32[]{:S(2)}) collective-permute-start(f32[2048,128]{1,0:T(8,128)S(1)} %bitcast.9), channel_id=1, source_target_pairs={{0,1},{1,0},{2,3},{3,2},{4,5},{5,4},{6,7},{7,6},{8,9},{9,8},{10,11... | collective-permute-start | bytes 3145736 | tf_op jit(solution)/shard_map/ppermute | solution.py:321

commit v5 on v4

--- a/solution.py
+++ b/solution.py
@@ -94,37 +94,55 @@
     return jnp.where(odd, pltpu.roll(value, 1, 1), pltpu.roll(value, 127, 1))
 
 
+def arrange(core, source_ref, tan_ref, flat, start, growth, growth_before):
+    for q in range(8):
+        block = source_ref[pl.ds(q, PANEL, stride=16), :].T
+        start[pl.ds(2 * q, 2)] = block.reshape(2, 8, 8, 128)
+        block = source_ref[pl.ds(8 + q, PANEL, stride=16), :].T
+        flat[pl.ds(q * 128, 128), :] = block
+    for y in range(HALF_ROWS // 2):
+        for x in range(8):
+            bond = (core * 16 + y) * 4 + x // 2
+            cos = jnp.where(tan_ref[0, bond] > 0.0, math.cosh(hop_angle), 1.0)
+            value = flat[pl.ds(y * LX + x, 8, stride=8), :] * cos
+            growth[y, x] = value
+            growth_before[y, x] = pltpu.roll(value, 126, 1)
+
+
+def arrange_kernel(own_ref, tan_ref, start, growth, growth_before, flat):
+    core = lax.axis_index("site") % 2
+    arrange(core, own_ref, tan_ref, flat, start, growth, growth_before)
+
+
 def solve_kernel(
-    sites_ref, own_ref, other_ref, tan_ref, mix_ref, out_ref,
+    sites_ref, own_start, own_growth, own_before, other_ref, tan_ref, mix_ref, out_ref,
     flat, growth, growth_before, gradient, history, image, edge, steps, betas,
 ):
     core = lax.axis_index("site") % 2
     column = 2 * lax.axis_index("tm") + lax.axis_index("site") // 2
     odd = lax.broadcasted_iota(jnp.int32, (8, 128), 1) % 2 == 1
 
-    for source_ref, place in ((own_ref, core), (other_ref, 1 - core)):
-        for q in range(8):
-            block = source_ref[pl.ds(q, PANEL, stride=16), :].T
-            gradient[pl.ds(place * 16 + 2 * q, 2)] = block.reshape(2, 8, 8, 128)
-            block = source_ref[pl.ds(8 + q, PANEL, stride=16), :].T
-            flat[pl.ds(place * 1024 + q * 128, 128), :] = block
+    for y in range(HALF_ROWS // 2):
+        own_y = core * 16 + y
+        for x in range(8):
+            gradient[own_y, x] = own_start[y, x]
+            growth[own_y, x] = own_growth[y, x]
+            growth_before[own_y, x] = own_before[y, x]
+    other_rows = pl.ds((1 - core) * 16, 16)
+    arrange(
+        1 - core, other_ref, tan_ref, flat,
+        gradient.at[other_rows], growth.at[other_rows], growth_before.at[other_rows],
+    )
     zero = jnp.zeros((8, 128), jnp.float32)
+    lane = lax.broadcasted_iota(jnp.int32, (8, 128), 1)
+    chosen = jnp.where(lane[:1] == column, sites_ref[...].astype(jnp.float32), 0.0)
+    site = jnp.sum(chosen, axis=1, keepdims=True).astype(jnp.int32)
+    beside = lane % 2 * (HALF_ROWS * LX) + lax.broadcasted_iota(jnp.int32, (8, 128), 0) * 8
+    wanted = jnp.where(lane // 2 == column * SLICES // PANEL, site - beside, -1)
     for y in range(HALF_ROWS):
         for x in range(8):
-            cos = jnp.where(tan_ref[0, y * 4 + x // 2] > 0.0, math.cosh(hop_angle), 1.0)
-            value = flat[pl.ds(y * LX + x, 8, stride=8), :] * cos
-            growth[y, x] = value
-            growth_before[y, x] = pltpu.roll(value, 126, 1)
-            image[y, x] = zero
+            image[y, x] = jnp.where(wanted == y * LX + x, 1.0, 0.0)
             history[ITERS + 1, y, x] = zero
-
-    site = sites_ref[column]
-    source_lane = 2 * (column * SLICES // PANEL) + site // (HALF_ROWS * LX)
-    source_x = site % LX
-    here = (lax.broadcasted_iota(jnp.int32, (8, 128), 0) == source_x // 8) & (
-        lax.broadcasted_iota(jnp.int32, (8, 128), 1) == source_lane
-    )
-    image[(site // LX) % HALF_ROWS, source_x % 8] = jnp.where(here, 1.0, 0.0)
 
     def along_x(row, y):
         row = list(row)
@@ -263,15 +281,12 @@
                     out_ref[pl.ds((2 * q + y) * LX + x, 8, stride=8), :] = block[8 * i : 8 * i + 8]
 
 
-def call(kernel, out_shape, scratch=(), smem_first=False, operands=1, cost=0):
+def call(kernel, out_shape, scratch=(), operands=1, cost=0):
     vmem = pl.BlockSpec(memory_space=pltpu.VMEM)
-    in_specs = [vmem] * operands
-    if smem_first:
-        in_specs[0] = pl.BlockSpec(memory_space=pltpu.SMEM)
     return pl.pallas_call(
         kernel,
         out_shape=out_shape,
-        in_specs=in_specs,
+        in_specs=[vmem] * operands,
         out_specs=jax.tree.map(lambda _: vmem, out_shape),
         scratch_shapes=list(scratch),
         compiler_params=pltpu.CompilerParams(vmem_limit_bytes=VMEM_LIMIT),
@@ -290,6 +305,8 @@
 
 
 def local_solve(source_sites, own, other, bonds):
+    flat = pltpu.VMEM((1024, 128), jnp.float32)
+    half = f32(HALF_ROWS // 2, 8, 8, 128)
     tan, mix = call(
         tables_kernel,
         (f32(3, 128, 8, 128), f32(4, 128, 8, 128)),
@@ -299,18 +316,21 @@
         ],
         cost=10_000_000,
     )(bonds)
+    arranged = call(arrange_kernel, (half, half, half), scratch=[flat], operands=2, cost=10_000_000)(
+        own, tan
+    )
     lattice = pltpu.VMEM((HALF_ROWS, 8, 8, 128), jnp.float32)
     return call(
         solve_kernel,
         f32(PANEL * 16, 128),
-        scratch=[pltpu.VMEM((2048, 128), jnp.float32)]
+        scratch=[flat]
         + [lattice] * 3
         + [pltpu.VMEM((ITERS + 2, HALF_ROWS, 8, 8, 128), jnp.float32)]
         + [lattice]
         + [pltpu.VMEM((8, 8, 128), jnp.float32)] * 3,
-        smem_first=True,
-        operands=5,
-    )(source_sites, own, other, tan, mix)
+
+        operands=7,
+    )(source_sites.reshape(1, PANEL), *arranged, other, tan, mix)
 
 
 def body(fields, bonds, source_sites, initial):
@@ -321,7 +341,10 @@
     other = lax.ppermute(own, AXES, CORE_SWAP)
     solved = local_solve(source_sites, own, other, bonds)
     arrived = exchange(solved)
-    solution, gradient = call(unpack_kernel, (f32(1024, PANEL), f32(1024, PANEL)))(arrived)
+    solution, gradient = call(
+        unpack_kernel,
+        (f32(1024, PANEL), f32(1024, PANEL)),
+    )(arrived)
     return solution.reshape(1, 1024, PANEL), gradient.reshape(1, 1024, PANEL)
 
 

time: 103 us -> 102 us (level)
    pallas_call x1 -> x2, Pallas kernels: 12.4 us -> 12.2 us  [the longest x1 11.7 us: local_solve(): call(solve_kernel, f32(PANEL * 16, 128), scratch=[flat] + [lattice] * 3 +...]
where the time goes in v5:
time: 102 us
  blocking collectives  83.1 us (81%)
  Pallas kernels  15 us (15%)
  local copies, waits for them, and re-layouts  1.73 us (2%)
  waiting for transfers between devices  1.15 us (1%)
    all_to_all x2, blocking collectives, exchange(): lax.all_to_all(parts, AXES, 0, 0, tiled=True, axis_index_groups=CORE_GROUPS)  83.1 us
    pallas_call x1, Pallas kernels, local_solve(): call(solve_kernel, f32(PANEL * 16, 128), scratch=[flat] + [lattice] * 3 +...  11.7 us
  transfers between devices with their start and end apart: 1, of which 1 were waited for; matrix products, arithmetic and copies ran while one was open for 0% of the time, Pallas kernels for 1%

profile of v5, /device:TPU:32, one launch (start us, length us, event | category | flops | bytes accessed | tf_op | source)
XLA Modules:
  0.0 101.7 jit_solution(5548579290283018948)
XLA Ops:
  0.6 0.0 copy-start
  0.6 1.0 %copy-done = f32[1,1024,128]{2,1,0:T(8,128)S(1)} copy-done((f32[1,1024,128]{2,1,0:T(8,128)S(1)}, f32[1,1024,128]{2,1,0:T(8,128)}, u32[]{:S(2)}) %copy-start) | copy-done | bytes 524312
  1.7 0.0 copy-start.1
  1.7 0.7 copy-done.1
  2.4 0.0 copy-start.3
  2.4 0.5 shard_map.59
  2.9 0.0 copy-start.2
  2.9 45.5 %all_to_all.10 = f32[128,16,128]{2,1,0:T(8,128)S(1)} all-to-all(f32[128,16,128]{2,1,0:T(8,128)S(1)} %bitcast.11), channel_id=1, replica_groups={{0,2,4,6,8,10,12,14,16,18,20,22,24,26,28,30,32,34,36,38,40,42,44,46,48,..., dimensions={0} | all-to-all | bytes 2097152 | tf_op jit(solution)/shard_map/all_to_all | solution.py:303
  48.4 0.0 collective-permute-start
  48.4 0.0 copy-done.3
  48.4 1.0 shard_map.60
  49.4 0.5 shard_map.61
  49.9 1.1 %collective-permute-done.other_ref = f32[2048,128]{1,0:T(8,128)S(1)} collective-permute-done((f32[2048,128]{1,0:T(8,128)S(1)}, f32[2048,128]{1,0:T(8,128)S(1)}, u32[]{:S(2)}, u32[]{:S(2)}) %collective-permute-start) | collective-permute-done | bytes 1048608 | tf_op jit(solution)/shard_map/ppermute | solution.py:341
  51.1 0.0 copy-done.2
  51.1 11.7 %shard_map.62 = f32[2048,128]{1,0:T(8,128)S(1)} custom-call(s32[1,128]{1,0:T(1,128)S(1)} %bitcast.14, f32[16,8,8,128]{3,2,1,0:T(8,128)S(1)} %get-tuple-element.10.own_start, f32[16,8,8,128]{3,2,1,0:T(8,128)S(1)} %get-tuple-element.11.own_growth, f32[16,8,8,128]{3,2,1,0:T(8,128)S(1)} %get-tuple-element.12.own_before, ...), custom_call_target="tpu_custom_call" | custom-call | bytes 1048576 | tf_op jit(solution)/shard_map/pallas_call | solution.py:323
  62.8 37.6 %all_to_all.11 = f32[128,16,128]{2,1,0:T(8,128)S(1)} all-to-all(f32[128,16,128]{2,1,0:T(8,128)S(1)} %bitcast.12), channel_id=1, replica_groups={{0,2,4,6,8,10,12,14,16,18,20,22,24,26,28,30,32,34,36,38,40,42,44,46,48,..., dimensions={0} | all-to-all | bytes 2097152 | tf_op jit(solution)/shard_map/all_to_all | solution.py:303
  100.3 1.3 %shard_map.63 = (f32[1024,128]{1,0:T(8,128)}, f32[1024,128]{1,0:T(8,128)}) custom-call(f32[2048,128]{1,0:T(8,128)S(1)} %bitcast.10), custom_call_target="tpu_custom_call" | custom-call | bytes 1048576 | tf_op jit(solution)/shard_map/pallas_call | solution.py:344
Async XLA Ops:
  0.6 1.0 %copy-start = (f32[1,1024,128]{2,1,0:T(8,128)S(1)}, f32[1,1024,128]{2,1,0:T(8,128)}, u32[]{:S(2)}) copy-start(f32[1,1024,128]{2,1,0:T(8,128)} %param.7) | copy-start | bytes 1572868
  1.7 0.7 copy-start.1
  2.4 46.1 %copy-start.3 = (s32[4,2048]{1,0:T(4,128)S(1)}, s32[4,2048]{1,0:T(4,128)}, u32[]{:S(2)}) copy-start(s32[4,2048]{1,0:T(4,128)} %bonds_ref.1) | copy-start | bytes 98308
  2.9 48.2 %copy-start.2 = (s32[128]{0:T(128)S(1)}, s32[128]{0:T(128)}, u32[]{:S(2)}) copy-start(s32[128]{0:T(128)} %param.6) | copy-start | bytes 1540
  48.4 2.7 %collective-permute-start = (f32[2048,128]{1,0:T(8,128)S(1)}, f32[2048,128]{1,0:T(8,128)S(1)}, u32[]{:S(2)}, u32[]{:S(2)}) collective-permute-start(f32[2048,128]{1,0:T(8,128)S(1)} %bitcast.8), channel_id=1, source_target_pairs={{0,1},{1,0},{2,3},{3,2},{4,5},{5,4},{6,7},{7,6},{8,9},{9,8},{10,11... | collective-permute-start | bytes 3145736 | tf_op jit(solution)/shard_map/ppermute | solution.py:341

commit v6 on v5

--- a/solution.py
+++ b/solution.py
@@ -28,8 +28,7 @@
 VMEM_LIMIT = 24 * 1024 * 1024
 
 
-def pack_kernel(initial_ref, fields_ref, out_ref):
-    sign = jnp.where(lax.axis_index("tm") == 0, 1.0, -1.0).astype(jnp.float32)
+def pack_kernel(initial_ref, growth_ref, out_ref):
     for q in range(8):
         rows = [
             initial_ref[pl.ds((2 * q + y) * LX + x, 8, stride=8), :]
@@ -37,8 +36,7 @@
             for x in range(8)
         ]
         out_ref[pl.ds(q, PANEL, stride=16), :] = jnp.concatenate(rows, axis=0).T
-        spin = fields_ref[:, q * 128 : (q + 1) * 128].astype(jnp.float32)
-        growth = sign * jnp.exp(coupling * (2.0 * spin - 1.0))
+        growth = growth_ref[:, q * 128 : (q + 1) * 128]
         out_ref[pl.ds(8 + q, PANEL, stride=16), :] = jnp.broadcast_to(growth, (PANEL, 128))
 
 
@@ -179,7 +177,7 @@
 
     def add_squares(totals, x, value):
         totals = list(totals)
-        totals[x % 4] = totals[x % 4] + value * value
+        totals[x] = totals[x] + value * value
         return totals
 
     def forward_pass(k, beta):
@@ -196,12 +194,12 @@
 
         def put(row, y, totals):
             for x in range(8):
-                value = (gradient[y, x] + pltpu.roll(row[x], 2, 1)) + beta * image[y, x]
+                value = (gradient[y, x] + beta * image[y, x]) + pltpu.roll(row[x], 2, 1)
                 image[y, x] = value
                 totals = add_squares(totals, x, value)
             return totals
 
-        totals = [zero] * 4
+        totals = [zero] * 8
         first, last = hopped(0)
         for x in range(8):
             edge[x] = first[x]
@@ -230,7 +228,7 @@
                     totals = add_squares(totals, x, value)
             return totals
 
-        totals = [zero] * 4
+        totals = [zero] * 8
         last, upper = across_halves(loaded(HALF_ROWS - 1), loaded(0))
         for x in range(8):
             edge[x] = last[x]
@@ -256,7 +254,7 @@
         return gamma, backward_pass(base, size)
 
     one = jnp.ones((8, 128), jnp.float32)
-    lax.fori_loop(0, ITERS + 1, turn, (jnp.ones((1, 1), jnp.float32), [one] * 4))
+    lax.fori_loop(0, ITERS + 1, turn, (jnp.ones((1, 1), jnp.float32), [one] * 8))
 
     weights = [steps[ITERS]]
     for k in range(ITERS - 1, 0, -1):
@@ -309,7 +307,7 @@
     half = f32(HALF_ROWS // 2, 8, 8, 128)
     tan, mix = call(
         tables_kernel,
-        (f32(3, 128, 8, 128), f32(4, 128, 8, 128)),
+        (f32(3, 129, 8, 128), f32(4, 129, 8, 128)),
         scratch=[
             pltpu.VMEM((4, 1024, 128), jnp.float32),
             pltpu.VMEM((2, 128, 8, 128), jnp.float32),
@@ -334,8 +332,10 @@
 
 
 def body(fields, bonds, source_sites, initial):
+    sign = jnp.where(lax.axis_index("tm") == 0, 1.0, -1.0).astype(jnp.float32)
+    growth = sign * jnp.exp(coupling * (2.0 * fields.astype(jnp.float32) - 1.0))
     packed = call(pack_kernel, f32(PANEL * 16, 128), operands=2)(
-        initial.reshape(1024, PANEL), fields
+        initial.reshape(1024, PANEL), growth
     )
     own = exchange(packed)
     other = lax.ppermute(own, AXES, CORE_SWAP)

time: 102 us -> 101 us (level)
  no operation moved by 1% of the time
where the time goes in v6:
time: 101 us
  blocking collectives  83.1 us (82%)
  Pallas kernels  14.5 us (14%)
  waiting for transfers between devices  1.15 us (1%)
  local copies, waits for them, and re-layouts  1.05 us (1%)
    all_to_all x2, blocking collectives, exchange(): lax.all_to_all(parts, AXES, 0, 0, tiled=True, axis_index_groups=CORE_GROUPS)  83.1 us
    pallas_call x1, Pallas kernels, local_solve(): call(solve_kernel, f32(PANEL * 16, 128), scratch=[flat] + [lattice] * 3 +...  11.2 us
  transfers between devices with their start and end apart: 1, of which 1 were waited for; matrix products, arithmetic and copies ran while one was open for 0% of the time, Pallas kernels for 1%

profile of v6, /device:TPU:32, one launch (start us, length us, event | category | flops | bytes accessed | tf_op | source)
XLA Modules:
  0.0 101.2 jit_solution(16679598230912704800)
XLA Ops:
  0.6 0.7 exponential_multiply_fusion.growth_ref
  1.3 0.0 copy-start
  1.4 1.0 %copy-done = f32[1,1024,128]{2,1,0:T(8,128)S(1)} copy-done((f32[1,1024,128]{2,1,0:T(8,128)S(1)}, f32[1,1024,128]{2,1,0:T(8,128)}, u32[]{:S(2)}) %copy-start) | copy-done | bytes 524312
  2.4 0.0 copy-start.2
  2.4 0.5 shard_map.59
  2.9 0.0 copy-start.1
  2.9 45.5 %all_to_all.10 = f32[128,16,128]{2,1,0:T(8,128)S(1)} all-to-all(f32[128,16,128]{2,1,0:T(8,128)S(1)} %bitcast.11), channel_id=1, replica_groups={{0,2,4,6,8,10,12,14,16,18,20,22,24,26,28,30,32,34,36,38,40,42,44,46,48,..., dimensions={0} | all-to-all | bytes 2097152 | tf_op jit(solution)/shard_map/all_to_all | solution.py:301
  48.4 0.0 collective-permute-start
  48.4 0.0 copy-done.2
  48.4 1.0 shard_map.60
  49.4 0.5 shard_map.61
  49.9 1.1 %collective-permute-done.other_ref = f32[2048,128]{1,0:T(8,128)S(1)} collective-permute-done((f32[2048,128]{1,0:T(8,128)S(1)}, f32[2048,128]{1,0:T(8,128)S(1)}, u32[]{:S(2)}, u32[]{:S(2)}) %collective-permute-start) | collective-permute-done | bytes 1048608 | tf_op jit(solution)/shard_map/ppermute | solution.py:341
  51.1 0.0 copy-done.1
  51.1 11.2 %shard_map.62 = f32[2048,128]{1,0:T(8,128)S(1)} custom-call(s32[1,128]{1,0:T(1,128)S(1)} %bitcast.14, f32[16,8,8,128]{3,2,1,0:T(8,128)S(1)} %get-tuple-element.10.own_start, f32[16,8,8,128]{3,2,1,0:T(8,128)S(1)} %get-tuple-element.11.own_growth, f32[16,8,8,128]{3,2,1,0:T(8,128)S(1)} %get-tuple-element.12.own_before, ...), custom_call_target="tpu_custom_call" | custom-call | bytes 1048576 | tf_op jit(solution)/shard_map/pallas_call | solution.py:321
  62.3 37.6 %all_to_all.11 = f32[128,16,128]{2,1,0:T(8,128)S(1)} all-to-all(f32[128,16,128]{2,1,0:T(8,128)S(1)} %bitcast.12), channel_id=1, replica_groups={{0,2,4,6,8,10,12,14,16,18,20,22,24,26,28,30,32,34,36,38,40,42,44,46,48,..., dimensions={0} | all-to-all | bytes 2097152 | tf_op jit(solution)/shard_map/all_to_all | solution.py:301
  99.9 1.3 %shard_map.63 = (f32[1024,128]{1,0:T(8,128)}, f32[1024,128]{1,0:T(8,128)}) custom-call(f32[2048,128]{1,0:T(8,128)S(1)} %bitcast.10), custom_call_target="tpu_custom_call" | custom-call | bytes 1048576 | tf_op jit(solution)/shard_map/pallas_call | solution.py:344
Async XLA Ops:
  1.3 1.0 %copy-start = (f32[1,1024,128]{2,1,0:T(8,128)S(1)}, f32[1,1024,128]{2,1,0:T(8,128)}, u32[]{:S(2)}) copy-start(f32[1,1024,128]{2,1,0:T(8,128)} %param.7) | copy-start | bytes 1572868
  2.4 46.0 %copy-start.2 = (s32[4,2048]{1,0:T(4,128)S(1)}, s32[4,2048]{1,0:T(4,128)}, u32[]{:S(2)}) copy-start(s32[4,2048]{1,0:T(4,128)} %bonds_ref.1) | copy-start | bytes 98308
  2.9 48.2 %copy-start.1 = (s32[128]{0:T(128)S(1)}, s32[128]{0:T(128)}, u32[]{:S(2)}) copy-start(s32[128]{0:T(128)} %param.6) | copy-start | bytes 1540
  48.4 2.7 %collective-permute-start = (f32[2048,128]{1,0:T(8,128)S(1)}, f32[2048,128]{1,0:T(8,128)S(1)}, u32[]{:S(2)}, u32[]{:S(2)}) collective-permute-start(f32[2048,128]{1,0:T(8,128)S(1)} %bitcast.8), channel_id=1, source_target_pairs={{0,1},{1,0},{2,3},{3,2},{4,5},{5,4},{6,7},{7,6},{8,9},{9,8},{10,11... | collective-permute-start | bytes 3145736 | tf_op jit(solution)/shard_map/ppermute | solution.py:341

commit v7 on v6

--- a/solution.py
+++ b/solution.py
@@ -114,7 +114,7 @@
 
 def solve_kernel(
     sites_ref, own_start, own_growth, own_before, other_ref, tan_ref, mix_ref, out_ref,
-    flat, growth, growth_before, gradient, history, image, edge, steps, betas,
+    flat, growth, growth_before, start, odd_turns, even_turns, image, edge, steps, betas,
 ):
     core = lax.axis_index("site") % 2
     column = 2 * lax.axis_index("tm") + lax.axis_index("site") // 2
@@ -123,13 +123,13 @@
     for y in range(HALF_ROWS // 2):
         own_y = core * 16 + y
         for x in range(8):
-            gradient[own_y, x] = own_start[y, x]
+            start[own_y, x] = own_start[y, x]
             growth[own_y, x] = own_growth[y, x]
             growth_before[own_y, x] = own_before[y, x]
     other_rows = pl.ds((1 - core) * 16, 16)
     arrange(
         1 - core, other_ref, tan_ref, flat,
-        gradient.at[other_rows], growth.at[other_rows], growth_before.at[other_rows],
+        start.at[other_rows], growth.at[other_rows], growth_before.at[other_rows],
     )
     zero = jnp.zeros((8, 128), jnp.float32)
     lane = lax.broadcasted_iota(jnp.int32, (8, 128), 1)
@@ -140,7 +140,6 @@
     for y in range(HALF_ROWS):
         for x in range(8):
             image[y, x] = jnp.where(wanted == y * LX + x, 1.0, 0.0)
-            history[ITERS + 1, y, x] = zero
 
     def along_x(row, y):
         row = list(row)
@@ -180,21 +179,19 @@
         totals[x] = totals[x] + value * value
         return totals
 
-    def forward_pass(k, beta):
+    def forward_pass(source, beta):
         def hopped(p):
             rows = []
             for y in (2 * p, 2 * p + 1):
                 row = []
                 for x in range(8):
-                    value = gradient[y, x]
-                    history[k, y, x] = value
-                    row.append(value * growth_before[y, x])
+                    row.append(source[y, x] * growth_before[y, x])
                 rows.append(along_x_shifted(along_x(row, y), y))
             return mixed(rows[0], rows[1], p, ((0, 1), (2, 3)))
 
         def put(row, y, totals):
             for x in range(8):
-                value = (gradient[y, x] + beta * image[y, x]) + pltpu.roll(row[x], 2, 1)
+                value = (source[y, x] + beta * image[y, x]) + pltpu.roll(row[x], 2, 1)
                 image[y, x] = value
                 totals = add_squares(totals, x, value)
             return totals
@@ -213,7 +210,7 @@
         totals = put(last, HALF_ROWS - 1, totals)
         return put(first, 0, totals)
 
-    def backward_pass(base, size):
+    def backward_pass(source, target, size):
         def loaded(y):
             return [image[y, x] for x in range(8)]
 
@@ -223,8 +220,8 @@
                 row = along_x(along_x_shifted(row, y), y)
                 for x in range(8):
                     value = image[y, x] + pltpu.roll(row[x] * growth[y, x], 126, 1)
-                    value = history[base, y, x] - size * value
-                    gradient[y, x] = value
+                    value = -value if source is None else source[y, x] - size * value
+                    target[y, x] = value
                     totals = add_squares(totals, x, value)
             return totals
 
@@ -241,31 +238,38 @@
     def whole(totals):
         return jnp.sum(sum(totals), keepdims=True)
 
-    def turn(k, carry):
+    def turn(k, source, target, gamma, beta):
+        size = gamma / whole(forward_pass(source, beta))
+        betas[k] = jnp.broadcast_to(beta, (8, 128))
+        steps[k] = jnp.broadcast_to(size, (8, 128))
+        return backward_pass(source, target, size)
+
+    def two_turns(j, carry):
         gamma_before, totals = carry
         gamma = whole(totals)
-        beta = jnp.where(k < 2, 0.0, gamma / gamma_before)
-        beta = jnp.where(k == 0, -1.0, beta)
-        squares = whole(forward_pass(k, beta))
-        size = jnp.where(k == 0, 1.0, gamma / squares)
-        betas[k] = jnp.broadcast_to(beta, (8, 128))
-        steps[k] = jnp.broadcast_to(size, (8, 128))
-        base = jnp.where(k == 0, ITERS + 1, k)
-        return gamma, backward_pass(base, size)
-
-    one = jnp.ones((8, 128), jnp.float32)
-    lax.fori_loop(0, ITERS + 1, turn, (jnp.ones((1, 1), jnp.float32), [one] * 8))
+        beta = jnp.where(j == 0, 0.0, gamma / gamma_before)
+        totals = turn(2 * j + 1, odd_turns.at[j], even_turns.at[j], gamma, beta)
+        gamma_next = whole(totals)
+        beta = gamma_next / gamma
+        return gamma_next, turn(
+            2 * j + 2, even_turns.at[j], odd_turns.at[j + 1], gamma_next, beta
+        )
+
+    forward_pass(start, -1.0)
+    totals = backward_pass(None, odd_turns.at[0], None)
+    lax.fori_loop(0, ITERS // 2, two_turns, (jnp.ones((1, 1), jnp.float32), totals))
 
     weights = [steps[ITERS]]
     for k in range(ITERS - 1, 0, -1):
         weights.insert(0, steps[k] + betas[k + 1] * weights[0])
     for q in range(8):
         mine = pl.ds(core * 16 + 2 * q, 2)
-        total = history[0, mine]
+        total = start[mine]
         for k in range(1, ITERS + 1):
-            total = total + weights[k - 1] * history[k, mine]
+            turns = odd_turns if k % 2 else even_turns
+            total = total + weights[k - 1] * turns[(k - 1) // 2, mine]
         out_ref[pl.ds(q, PANEL, stride=16), :] = total.reshape(128, 128).T
-        block = gradient[mine].reshape(128, 128)
+        block = odd_turns[ITERS // 2, mine].reshape(128, 128)
         out_ref[pl.ds(8 + q, PANEL, stride=16), :] = block.T
 
 
@@ -323,10 +327,9 @@
         f32(PANEL * 16, 128),
         scratch=[flat]
         + [lattice] * 3
-        + [pltpu.VMEM((ITERS + 2, HALF_ROWS, 8, 8, 128), jnp.float32)]
+        + [pltpu.VMEM((n, HALF_ROWS, 8, 8, 128), jnp.float32) for n in (ITERS // 2 + 1, ITERS // 2)]
         + [lattice]
         + [pltpu.VMEM((8, 8, 128), jnp.float32)] * 3,
-
         operands=7,
     )(source_sites.reshape(1, PANEL), *arranged, other, tan, mix)
 

time: 101 us -> 101 us (level)
  no operation moved by 1% of the time
where the time goes in v7:
time: 101 us
  blocking collectives  83.1 us (82%)
  Pallas kernels  14.3 us (14%)
  waiting for transfers between devices  1.15 us (1%)
  local copies, waits for them, and re-layouts  1.05 us (1%)
    all_to_all x2, blocking collectives, exchange(): lax.all_to_all(parts, AXES, 0, 0, tiled=True, axis_index_groups=CORE_GROUPS)  83.1 us
    pallas_call x1, Pallas kernels, local_solve(): call(solve_kernel, f32(PANEL * 16, 128), scratch=[flat] + [lattice] * 3 +...  11 us
  transfers between devices with their start and end apart: 1, of which 1 were waited for; matrix products, arithmetic and copies ran while one was open for 0% of the time, Pallas kernels for 1%

profile of v7, /device:TPU:32, one launch (start us, length us, event | category | flops | bytes accessed | tf_op | source)
XLA Modules:
  0.0 101.0 jit_solution(7818856218216492889)
XLA Ops:
  0.6 0.7 exponential_multiply_fusion.growth_ref
  1.3 0.0 copy-start
  1.4 1.0 %copy-done = f32[1,1024,128]{2,1,0:T(8,128)S(1)} copy-done((f32[1,1024,128]{2,1,0:T(8,128)S(1)}, f32[1,1024,128]{2,1,0:T(8,128)}, u32[]{:S(2)}) %copy-start) | copy-done | bytes 524312
  2.4 0.0 copy-start.2
  2.4 0.5 shard_map.59
  2.9 0.0 copy-start.1
  2.9 45.5 %all_to_all.10 = f32[128,16,128]{2,1,0:T(8,128)S(1)} all-to-all(f32[128,16,128]{2,1,0:T(8,128)S(1)} %bitcast.11), channel_id=1, replica_groups={{0,2,4,6,8,10,12,14,16,18,20,22,24,26,28,30,32,34,36,38,40,42,44,46,48,..., dimensions={0} | all-to-all | bytes 2097152 | tf_op jit(solution)/shard_map/all_to_all | solution.py:305
  48.4 0.0 collective-permute-start
  48.4 0.0 copy-done.2
  48.4 1.0 shard_map.60
  49.4 0.5 shard_map.61
  49.9 1.1 %collective-permute-done.other_ref = f32[2048,128]{1,0:T(8,128)S(1)} collective-permute-done((f32[2048,128]{1,0:T(8,128)S(1)}, f32[2048,128]{1,0:T(8,128)S(1)}, u32[]{:S(2)}, u32[]{:S(2)}) %collective-permute-start) | collective-permute-done | bytes 1048608 | tf_op jit(solution)/shard_map/ppermute | solution.py:344
  51.1 0.0 copy-done.1
  51.1 11.0 %shard_map.62 = f32[2048,128]{1,0:T(8,128)S(1)} custom-call(s32[1,128]{1,0:T(1,128)S(1)} %bitcast.14, f32[16,8,8,128]{3,2,1,0:T(8,128)S(1)} %get-tuple-element.10.own_start, f32[16,8,8,128]{3,2,1,0:T(8,128)S(1)} %get-tuple-element.11.own_growth, f32[16,8,8,128]{3,2,1,0:T(8,128)S(1)} %get-tuple-element.12.own_before, ...), custom_call_target="tpu_custom_call" | custom-call | bytes 1048576 | tf_op jit(solution)/shard_map/pallas_call | solution.py:325
  62.1 37.6 %all_to_all.11 = f32[128,16,128]{2,1,0:T(8,128)S(1)} all-to-all(f32[128,16,128]{2,1,0:T(8,128)S(1)} %bitcast.12), channel_id=1, replica_groups={{0,2,4,6,8,10,12,14,16,18,20,22,24,26,28,30,32,34,36,38,40,42,44,46,48,..., dimensions={0} | all-to-all | bytes 2097152 | tf_op jit(solution)/shard_map/all_to_all | solution.py:305
  99.7 1.3 %shard_map.63 = (f32[1024,128]{1,0:T(8,128)}, f32[1024,128]{1,0:T(8,128)}) custom-call(f32[2048,128]{1,0:T(8,128)S(1)} %bitcast.10), custom_call_target="tpu_custom_call" | custom-call | bytes 1048576 | tf_op jit(solution)/shard_map/pallas_call | solution.py:347
Async XLA Ops:
  1.3 1.0 %copy-start = (f32[1,1024,128]{2,1,0:T(8,128)S(1)}, f32[1,1024,128]{2,1,0:T(8,128)}, u32[]{:S(2)}) copy-start(f32[1,1024,128]{2,1,0:T(8,128)} %param.7) | copy-start | bytes 1572868
  2.4 46.0 %copy-start.2 = (s32[4,2048]{1,0:T(4,128)S(1)}, s32[4,2048]{1,0:T(4,128)}, u32[]{:S(2)}) copy-start(s32[4,2048]{1,0:T(4,128)} %bonds_ref.1) | copy-start | bytes 98308
  2.9 48.2 %copy-start.1 = (s32[128]{0:T(128)S(1)}, s32[128]{0:T(128)}, u32[]{:S(2)}) copy-start(s32[128]{0:T(128)} %param.6) | copy-start | bytes 1540
  48.4 2.7 %collective-permute-start = (f32[2048,128]{1,0:T(8,128)S(1)}, f32[2048,128]{1,0:T(8,128)S(1)}, u32[]{:S(2)}, u32[]{:S(2)}) collective-permute-start(f32[2048,128]{1,0:T(8,128)S(1)} %bitcast.8), channel_id=1, source_target_pairs={{0,1},{1,0},{2,3},{3,2},{4,5},{5,4},{6,7},{7,6},{8,9},{9,8},{10,11... | collective-permute-start | bytes 3145736 | tf_op jit(solution)/shard_map/ppermute | solution.py:344

commit v8 on v7

--- a/solution.py
+++ b/solution.py
@@ -273,23 +273,31 @@
         out_ref[pl.ds(8 + q, PANEL, stride=16), :] = block.T
 
 
-def unpack_kernel(arrived_ref, solution_ref, gradient_ref):
-    for part, out_ref in enumerate((solution_ref, gradient_ref)):
-        for q in range(8):
+def unpack_kernel(arrived_ref, solution_hbm, gradient_hbm, solution_ref, gradient_ref, sent):
+    copies = []
+    for q in range(8):
+        for part, (ref, hbm) in enumerate(
+            ((solution_ref, solution_hbm), (gradient_ref, gradient_hbm))
+        ):
             block = arrived_ref[pl.ds(8 * part + q, PANEL, stride=16), :].T
             for y in range(2):
                 for x in range(8):
                     i = y * 8 + x
-                    out_ref[pl.ds((2 * q + y) * LX + x, 8, stride=8), :] = block[8 * i : 8 * i + 8]
-
-
-def call(kernel, out_shape, scratch=(), operands=1, cost=0):
+                    ref[pl.ds((2 * q + y) * LX + x, 8, stride=8), :] = block[8 * i : 8 * i + 8]
+            rows = pl.ds(q * 128, 128)
+            copies.append(pltpu.make_async_copy(ref.at[rows], hbm.at[rows], sent.at[part, q]))
+            copies[-1].start()
+    for copy in copies:
+        copy.wait()
+
+
+def call(kernel, out_shape, scratch=(), operands=1, cost=0, out_space=pltpu.VMEM):
     vmem = pl.BlockSpec(memory_space=pltpu.VMEM)
     return pl.pallas_call(
         kernel,
         out_shape=out_shape,
         in_specs=[vmem] * operands,
-        out_specs=jax.tree.map(lambda _: vmem, out_shape),
+        out_specs=jax.tree.map(lambda _: pl.BlockSpec(memory_space=out_space), out_shape),
         scratch_shapes=list(scratch),
         compiler_params=pltpu.CompilerParams(vmem_limit_bytes=VMEM_LIMIT),
         cost_estimate=pl.CostEstimate(flops=cost, bytes_accessed=1 << 20, transcendentals=0),
@@ -344,9 +352,12 @@
     other = lax.ppermute(own, AXES, CORE_SWAP)
     solved = local_solve(source_sites, own, other, bonds)
     arrived = exchange(solved)
+    block = pltpu.VMEM((1024, PANEL), jnp.float32)
     solution, gradient = call(
         unpack_kernel,
         (f32(1024, PANEL), f32(1024, PANEL)),
+        scratch=[block, block, pltpu.SemaphoreType.DMA((2, 8))],
+        out_space=pl.ANY,
     )(arrived)
     return solution.reshape(1, 1024, PANEL), gradient.reshape(1, 1024, PANEL)
 

time: 101 us -> 101 us (level)
  no operation moved by 1% of the time
where the time goes in v8:
time: 101 us
  blocking collectives  83.1 us (82%)
  Pallas kernels  14.3 us (14%)
  waiting for transfers between devices  1.15 us (1%)
  local copies, waits for them, and re-layouts  1.05 us (1%)
    all_to_all x2, blocking collectives, exchange(): lax.all_to_all(parts, AXES, 0, 0, tiled=True, axis_index_groups=CORE_GROUPS)  83.1 us
    pallas_call x1, Pallas kernels, local_solve(): call(solve_kernel, f32(PANEL * 16, 128), scratch=[flat] + [lattice] * 3 +...  11 us
  transfers between devices with their start and end apart: 1, of which 1 were waited for; matrix products, arithmetic and copies ran while one was open for 0% of the time, Pallas kernels for 1%

profile of v8, /device:TPU:32, one launch (start us, length us, event | category | flops | bytes accessed | tf_op | source)
XLA Modules:
  0.0 100.9 jit_solution(12710323058243919918)
XLA Ops:
  0.6 0.7 exponential_multiply_fusion.growth_ref
  1.3 0.0 copy-start
  1.4 1.0 %copy-done = f32[1,1024,128]{2,1,0:T(8,128)S(1)} copy-done((f32[1,1024,128]{2,1,0:T(8,128)S(1)}, f32[1,1024,128]{2,1,0:T(8,128)}, u32[]{:S(2)}) %copy-start) | copy-done | bytes 524312
  2.4 0.0 copy-start.2
  2.4 0.5 shard_map.59
  2.9 0.0 copy-start.1
  2.9 45.5 %all_to_all.10 = f32[128,16,128]{2,1,0:T(8,128)S(1)} all-to-all(f32[128,16,128]{2,1,0:T(8,128)S(1)} %bitcast.11), channel_id=1, replica_groups={{0,2,4,6,8,10,12,14,16,18,20,22,24,26,28,30,32,34,36,38,40,42,44,46,48,..., dimensions={0} | all-to-all | bytes 2097152 | tf_op jit(solution)/shard_map/all_to_all | solution.py:313
  48.4 0.0 collective-permute-start
  48.4 0.0 copy-done.2
  48.4 1.0 shard_map.60
  49.4 0.5 shard_map.61
  49.9 1.1 %collective-permute-done.other_ref = f32[2048,128]{1,0:T(8,128)S(1)} collective-permute-done((f32[2048,128]{1,0:T(8,128)S(1)}, f32[2048,128]{1,0:T(8,128)S(1)}, u32[]{:S(2)}, u32[]{:S(2)}) %collective-permute-start) | collective-permute-done | bytes 1048608 | tf_op jit(solution)/shard_map/ppermute | solution.py:352
  51.1 0.0 copy-done.1
  51.1 11.0 %shard_map.62 = f32[2048,128]{1,0:T(8,128)S(1)} custom-call(s32[1,128]{1,0:T(1,128)S(1)} %bitcast.14, f32[16,8,8,128]{3,2,1,0:T(8,128)S(1)} %get-tuple-element.10.own_start, f32[16,8,8,128]{3,2,1,0:T(8,128)S(1)} %get-tuple-element.11.own_growth, f32[16,8,8,128]{3,2,1,0:T(8,128)S(1)} %get-tuple-element.12.own_before, ...), custom_call_target="tpu_custom_call" | custom-call | bytes 1048576 | tf_op jit(solution)/shard_map/pallas_call | solution.py:333
  62.1 37.6 %all_to_all.11 = f32[128,16,128]{2,1,0:T(8,128)S(1)} all-to-all(f32[128,16,128]{2,1,0:T(8,128)S(1)} %bitcast.12), channel_id=1, replica_groups={{0,2,4,6,8,10,12,14,16,18,20,22,24,26,28,30,32,34,36,38,40,42,44,46,48,..., dimensions={0} | all-to-all | bytes 2097152 | tf_op jit(solution)/shard_map/all_to_all | solution.py:313
  99.7 1.3 %shard_map.63 = (f32[1024,128]{1,0:T(8,128)}, f32[1024,128]{1,0:T(8,128)}) custom-call(f32[2048,128]{1,0:T(8,128)S(1)} %bitcast.10), custom_call_target="tpu_custom_call" | custom-call | bytes 1048576 | tf_op jit(solution)/shard_map/pallas_call | solution.py:356
Async XLA Ops:
  1.3 1.0 %copy-start = (f32[1,1024,128]{2,1,0:T(8,128)S(1)}, f32[1,1024,128]{2,1,0:T(8,128)}, u32[]{:S(2)}) copy-start(f32[1,1024,128]{2,1,0:T(8,128)} %param.7) | copy-start | bytes 1572868
  2.4 46.0 %copy-start.2 = (s32[4,2048]{1,0:T(4,128)S(1)}, s32[4,2048]{1,0:T(4,128)}, u32[]{:S(2)}) copy-start(s32[4,2048]{1,0:T(4,128)} %bonds_ref.1) | copy-start | bytes 98308
  2.9 48.2 %copy-start.1 = (s32[128]{0:T(128)S(1)}, s32[128]{0:T(128)}, u32[]{:S(2)}) copy-start(s32[128]{0:T(128)} %param.6) | copy-start | bytes 1540
  48.4 2.7 %collective-permute-start = (f32[2048,128]{1,0:T(8,128)S(1)}, f32[2048,128]{1,0:T(8,128)S(1)}, u32[]{:S(2)}, u32[]{:S(2)}) collective-permute-start(f32[2048,128]{1,0:T(8,128)S(1)} %bitcast.8), channel_id=1, source_target_pairs={{0,1},{1,0},{2,3},{3,2},{4,5},{5,4},{6,7},{7,6},{8,9},{9,8},{10,11... | collective-permute-start | bytes 3145736 | tf_op jit(solution)/shard_map/ppermute | solution.py:352
